TPU v7x, 256 devices: a whole 4x4x8 slice. The times are simulated.
256 devices in a mesh: patch: 64 (over y, z, core), grp: 4 (over x).
Axes of the slice: x: 4, y: 4, z: 8, core: 2. Of those that a mesh axis runs over, the one named last changes fastest.
Arguments:
- sky: bfloat16 [131072, 1024], P(('patch', 'grp')), may hold values from -24 to 24
- send_index: int32 [64, 4, 64, 32], P('patch', 'grp'), may hold values from 0 to 511, as said below
- send_count: int32 [64, 4, 64], P('patch', 'grp'), may hold values from 0 to 32, as said below
- taper: float32 [64, 4, 64, 32], P('patch', 'grp'), may hold values from 0.1 to 1
- start_basis: float32 [1024, 12], replicated, may hold values from -0.1875 to 0.1875
Outputs:
- cleaned_sky: float32 [131072, 1024], P(('patch', 'grp'))
Inputs may be any that keep to these rules, and one draw needn't show every extreme that they name: `send_index`: within one list the first send_count entries are distinct. `send_count`: in every draw some patch receives 32 rows from every device.
All inputs are finite; a program needn't handle non-finite values.
Results may differ from a plain program's by a relative error of at most 0.0055.
Values may be sent and summed in bfloat16 or wider, within the bound.
A program may use at most 64 MiB of HBM per device.

v0:
```python
import jax
import jax.numpy as jnp
from jax import lax
from jax.sharding import PartitionSpec as P

ITERS = 6


def orthonormal(matrix):
    columns = []
    for column_index in range(matrix.shape[1]):
        vector = matrix[:, column_index]
        for earlier in columns:
            vector = vector - jnp.sum(earlier * vector) * earlier
        vector = vector / jnp.sqrt(jnp.sum(vector * vector) + 1e-12)
        columns.append(vector)
    return jnp.stack(columns, axis=1)


def local(sky, send_index, send_count, taper, start_basis):
    highest = lax.Precision.HIGHEST
    patch_count = send_index.shape[2]
    capacity = send_index.shape[3]
    channels = sky.shape[1]
    local_rows = send_index.reshape(patch_count, capacity)
    live_slots = jnp.arange(capacity)[None, :] < send_count.reshape(patch_count)[:, None]
    outgoing = jnp.where(live_slots[:, :, None], sky[local_rows], jnp.zeros((), sky.dtype))
    received = lax.all_to_all(outgoing, "patch", split_axis=0, concat_axis=0, tiled=True)
    slot_rows = received.reshape(-1, channels)
    gram_local = jnp.einsum("rf,rg->fg", slot_rows, slot_rows, preferred_element_type=jnp.float32)
    gram_matrix = lax.psum(gram_local, "grp")
    subspace = start_basis
    for sweep in range(ITERS):
        subspace = orthonormal(jnp.dot(gram_matrix, subspace, precision=highest))
    basis_low = subspace.astype(jnp.bfloat16)
    coefficients = jnp.dot(slot_rows, basis_low, preferred_element_type=jnp.float32)
    cleaned = (
        slot_rows.astype(jnp.float32)
        - jnp.dot(coefficients, basis_low.astype(jnp.float32).T, precision=highest)
    ).astype(jnp.bfloat16)
    returned = lax.all_to_all(
        cleaned.reshape(patch_count, capacity, channels),
        "patch",
        split_axis=0,
        concat_axis=0,
        tiled=True,
    )
    weights = jnp.where(
        live_slots, taper.reshape(patch_count, capacity), jnp.zeros((), taper.dtype)
    )
    flat_rows = local_rows.reshape(-1)
    numerator = (
        jnp.zeros((sky.shape[0], channels), jnp.float32)
        .at[flat_rows]
        .add((weights[:, :, None] * returned.astype(jnp.float32)).reshape(-1, channels))
    )
    weight_total = jnp.zeros((sky.shape[0],), jnp.float32).at[flat_rows].add(weights.reshape(-1))
    covered = weight_total > 0
    safe_total = jnp.where(covered, weight_total, jnp.ones((), jnp.float32))
    return jnp.where(covered[:, None], numerator / safe_total[:, None], sky.astype(jnp.float32))


def solution(mesh):
    placed = (
        P(("patch", "grp"), None),
        P("patch", "grp", None, None),
        P("patch", "grp", None),
        P("patch", "grp", None, None),
        P(),
    )
    return jax.shard_map(
        local, mesh=mesh, in_specs=placed, out_specs=P(("patch", "grp"), None), check_vma=False
    )
```

profile of v0, /device:TPU:1, one launch (start us, length us, event | category | flops | bytes accessed | tf_op | source)
XLA Modules:
  0.0 1207.5 jit_solution(12880805913933181035)
XLA Ops:
  8.2 12.4 %gather_fusion = bf16[2048,1024]{1,0:T(8,128)(2,1)} fusion(bf16[512,1024]{1,0:T(8,128)(2,1)} %param.5, s32[2048]{0:T(1024)S(1)} %broadcast_clamp_fusion), kind=kCustom, calls=%fused_computation | custom fusion | bytes 8396800 | tf_op jit(solution)/shard_map/gather | solution.py:27
  23.1 109.1 %all_to_all.10 = bf16[64,32,1024]{2,1,0:T(8,128)(2,1)S(1)} all-to-all(bf16[64,32,1024]{2,1,0:T(8,128)(2,1)S(1)} %broadcast_select_fusion), channel_id=1, replica_groups=mesh['patch'=64,'grp'=4] {'patch'}, dimensions={0} | all-to-all | bytes 8388608 | tf_op jit(solution)/shard_map/all_to_all | solution.py:28
  134.1 6.6 convolution_bitcast_fusion
  140.8 94.5 %all-reduce.2.cloned.1.call-done = f32[1024,1024]{1,0:T(8,128)} async-done(((f32[1024,1024]{1,0:T(8,128)}), f32[1024,1024]{1,0:T(8,128)}) %all-reduce.2.cloned.1.call-update) | async-done | bytes 4194320 | tf_op jit(solution)/shard_map/psum | solution.py:31
  235.3 5.8 fusion.10
  245.0 6.2 multiply_reduce_fusion.400
  257.4 11.2 multiply_reduce_fusion.399
  269.2 6.3 multiply_reduce_fusion.398
  279.9 8.6 multiply_reduce_fusion.397
  289.2 4.8 multiply_reduce_fusion.396
  298.5 6.3 multiply_reduce_fusion.395
  315.2 4.5 multiply_reduce_fusion.393
  331.1 41.0 %subtract_divide_fusion.54 = (f32[1024,1]{0,1:T(1,128)S(1)}, f32[1024,1]{0,1:T(1,128)S(1)}, f32[1024,1]{0,1:T(1,128)S(1)}, f32[1024,1]{0,1:T(1,128)S(1)}, f32[10...) fusion(f32[1024,1]{0,1:T(1,128)S(1)} %get-tuple-element.793, ...), kind=kLoop, calls=%fused_computation.786 | loop fusion | flops 146432 | bytes 94516 | tf_op jit(solution)/shard_map/div | solution.py:15
  372.2 5.8 fusion.11
  381.9 6.2 multiply_reduce_fusion.322
  394.3 11.2 multiply_reduce_fusion.321
  406.2 6.3 multiply_reduce_fusion.320
  416.8 8.6 multiply_reduce_fusion.319
  426.2 4.8 multiply_reduce_fusion.318
  435.4 6.3 multiply_reduce_fusion.317
  452.1 4.5 multiply_reduce_fusion.315
  468.0 41.0 %subtract_divide_fusion.43 = (f32[1024,1]{0,1:T(1,128)S(1)}, f32[1024,1]{0,1:T(1,128)S(1)}, f32[1024,1]{0,1:T(1,128)S(1)}, f32[1024,1]{0,1:T(1,128)S(1)}, f32[10...) fusion(f32[1024,1]{0,1:T(1,128)S(1)} %get-tuple-element.781, ...), kind=kLoop, calls=%fused_computation.632 | loop fusion | flops 146432 | bytes 94516 | tf_op jit(solution)/shard_map/div | solution.py:15
  509.2 5.9 fusion.12
  519.0 6.2 multiply_reduce_fusion.244
  531.4 11.2 multiply_reduce_fusion.243
  543.3 6.3 multiply_reduce_fusion.242
  553.9 8.6 multiply_reduce_fusion.241
  563.3 4.8 multiply_reduce_fusion.240
  572.5 6.3 multiply_reduce_fusion.239
  589.2 4.5 multiply_reduce_fusion.237
  605.1 41.0 %subtract_divide_fusion.32 = (f32[1024,1]{0,1:T(1,128)S(1)}, f32[1024,1]{0,1:T(1,128)S(1)}, f32[1024,1]{0,1:T(1,128)S(1)}, f32[1024,1]{0,1:T(1,128)S(1)}, f32[10...) fusion(f32[1024,1]{0,1:T(1,128)S(1)} %get-tuple-element.769, ...), kind=kLoop, calls=%fused_computation.478 | loop fusion | flops 146432 | bytes 94516 | tf_op jit(solution)/shard_map/div | solution.py:15
  646.3 5.8 fusion.13
  656.0 6.2 multiply_reduce_fusion.166
  668.4 11.2 multiply_reduce_fusion.165
  680.2 6.3 multiply_reduce_fusion.164
  690.9 8.6 multiply_reduce_fusion.163
  700.2 4.8 multiply_reduce_fusion.162
  709.5 6.3 multiply_reduce_fusion.161
  726.2 4.5 multiply_reduce_fusion.159
  742.1 41.0 %subtract_divide_fusion.21 = (f32[1024,1]{0,1:T(1,128)S(1)}, f32[1024,1]{0,1:T(1,128)S(1)}, f32[1024,1]{0,1:T(1,128)S(1)}, f32[1024,1]{0,1:T(1,128)S(1)}, f32[10...) fusion(f32[1024,1]{0,1:T(1,128)S(1)} %get-tuple-element.757, ...), kind=kLoop, calls=%fused_computation.324 | loop fusion | flops 146432 | bytes 94516 | tf_op jit(solution)/shard_map/div | solution.py:15
  783.2 5.8 fusion.14
  792.9 6.2 multiply_reduce_fusion.88
  805.3 11.2 multiply_reduce_fusion.87
  817.2 6.3 multiply_reduce_fusion.86
  827.8 8.6 multiply_reduce_fusion.85
  837.1 4.8 multiply_reduce_fusion.84
  846.4 6.3 multiply_reduce_fusion.83
  863.1 4.5 multiply_reduce_fusion.81
  879.0 41.0 %subtract_divide_fusion.10 = (f32[1024,1]{0,1:T(1,128)S(1)}, f32[1024,1]{0,1:T(1,128)S(1)}, f32[1024,1]{0,1:T(1,128)S(1)}, f32[1024,1]{0,1:T(1,128)S(1)}, f32[10...) fusion(f32[1024,1]{0,1:T(1,128)S(1)} %get-tuple-element.745, ...), kind=kLoop, calls=%fused_computation.170 | loop fusion | flops 146432 | bytes 94516 | tf_op jit(solution)/shard_map/div | solution.py:15
  920.1 6.0 fusion.15
  930.1 6.3 multiply_reduce_fusion.10
  942.8 11.2 multiply_reduce_fusion.9
  954.6 6.4 multiply_reduce_fusion.8
  965.4 8.9 multiply_reduce_fusion.7
  974.9 5.2 multiply_reduce_fusion.6
  984.3 6.4 multiply_reduce_fusion.5
  1000.6 4.3 multiply_reduce_fusion.3
  1015.8 41.5 %divide_convert_fusion = (bf16[1024,1]{0,1:T(2,128)(2,1)S(1)}, bf16[1024,1]{0,1:T(2,128)(2,1)S(1)}, bf16[1024,1]{0,1:T(2,128)(2,1)S(1)}, bf16[1024,1]{0,1:T(2,12...) fusion(f32[1024,1]{0,1:T(1,128)S(1)} %get-tuple-element.452, ...), kind=kLoop, calls=%fused_computation.15 | loop fusion | flops 157696 | bytes 71988 | tf_op jit(solution)/shard_map/convert.11
  1060.9 5.2 subtract_convert_fusion
  1066.1 11.0 all-to-all-start.1
  1077.7 14.7 %scatter_custom_fusion = f32[512]{0:T(512)S(1)} fusion(s32[2048]{0:T(1024)S(1)} %bitcast.353, f32[2048]{0:T(1024)S(1)} %broadcast_select_fusion.1, f32[]{:T(128)} %constant.6.clone.1), kind=kCustom, calls=%fused_computation.1008 | custom fusion | flops 2048 | bytes 2052 | tf_op jit(solution)/shard_map/scatter-add | solution.py:57
  1092.4 80.6 %all-to-all-done.1 = bf16[64,32,1024]{2,1,0:T(8,128)(2,1)} async-done(((bf16[64,32,1024]{2,1,0:T(8,128)(2,1)}), bf16[64,32,1024]{2,1,0:T(8,128)(2,1)}, u32[]{:S(2)}, u32[]{:S(2)}) %all-to-all-start.1) | async-done | bytes 4194336 | tf_op jit(solution)/shard_map/all_to_all | solution.py:41
  1173.0 6.0 convert_multiply_fusion
  1179.0 19.7 %scatter_custom_fusion.1 = f32[512,1024]{1,0:T(8,128)S(1)} fusion(s32[2048]{0:T(1024)S(1)} %bitcast.354, f32[2048,1024]{1,0:T(8,128)} %bitcast.112, f32[]{:T(128)} %constant.6.clone.1), kind=kCustom, calls=%fused_computation.8 | custom fusion | flops 2097152 | bytes 2097664 | tf_op jit(solution)/shard_map/scatter-add | solution.py:55
  (150 shorter events, 214.8 us)
Async XLA Ops:
  6.5 228.7 %copy-start = (f32[1024,12]{0,1:T(8,128)S(1)}, f32[1024,12]{0,1:T(8,128)}, u32[]{:S(2)}) copy-start(f32[1024,12]{0,1:T(8,128)} %param.9) | copy-start | bytes 147460
  6.5 228.7 %all-reduce.2.cloned.1.call-start = ((), (), s32[]{:S(2)}) async-start(), calls=%async_computation.2 | async-start | bytes 8388608 | tf_op jit(solution)/shard_map/psum | solution.py:31
  132.2 1.9 copy-start.2
  1057.4 3.5 copy-start.3
  1066.1 11.0 copy-start.4
  1066.1 11.2 copy-start.5
  1066.1 11.3 copy-start.6
  1066.1 106.9 %all-to-all-start.1 = ((bf16[64,32,1024]{2,1,0:T(8,128)(2,1)}), bf16[64,32,1024]{2,1,0:T(8,128)(2,1)}, u32[]{:S(2)}, u32[]{:S(2)}) async-start(bf16[64,32,1024]{2,1,0:T(8,128)(2,1)} %bitcast.110), calls=%async_computation.1 | async-start | bytes 8388608 | tf_op jit(solution)/shard_map/all_to_all | solution.py:41
  1092.4 106.4 %copy-start.1 = (bf16[512,1024]{1,0:T(8,128)(2,1)S(1)}, bf16[512,1024]{1,0:T(8,128)(2,1)}, u32[]{:S(2)}) copy-start(bf16[512,1024]{1,0:T(8,128)(2,1)} %param.5) | copy-start | bytes 3145732
Sparse Core Ops, SparseCore 0:
  140.9 94.3 all-reduce.1
where the time goes:
time: 1220 us; the launch traced here: 1210 us
  other arithmetic  783 us (64%)
  waiting for transfers between devices  175 us (14%)
  blocking collectives  109 us (9%)
  between operations  63.4 us (5%)
  matrix products  50.2 us (4%)
  local copies, waits for them, and re-layouts  15.6 us (1%)
    reduce_sum x102, other arithmetic, orthonormal(): vector = vector - jnp.sum(earlier * vector) * earlier  414 us
    div x5, other arithmetic, orthonormal(): vector = vector / jnp.sqrt(jnp.sum(vector * vector) + 1e-12)  205 us
    all_to_all x1, blocking collectives, local(): lax.all_to_all(outgoing, 'patch', split_axis=0, concat_axis=0, tiled=True)  109 us
    psum x1, waiting for transfers between devices, local(): gram_matrix = lax.psum(gram_local, 'grp')  94.5 us
    all_to_all x1, waiting for transfers between devices, local(): lax.all_to_all(cleaned.reshape(patch_count, capacity, channels), 'patch',...  80.6 us
    reduce_sum x42, other arithmetic, orthonormal(): vector = vector / jnp.sqrt(jnp.sum(vector * vector) + 1e-12)  76.5 us
    another operation x2, other arithmetic  41.5 us
    dot_general x6, matrix products, local(): subspace = orthonormal(jnp.dot(gram_matrix, subspace, precision=highest))  34.9 us
  transfers between devices with their start and end apart: 2, of which 2 were waited for; matrix products, arithmetic and copies ran while one was open for 1% of the time, Pallas kernels for 0%

commit v1 on v0

v1 whole, which is shorter than its diff:
```python
import jax
import jax.numpy as jnp
from jax import lax
from jax.experimental import pallas as pl
from jax.experimental.pallas import tpu as pltpu
from jax.sharding import Mesh, PartitionSpec as P

ITERS = 6
MODES = 12
SHARERS = 4
PAD = 16
CELL = ("y", "core", "x", "zl")
MESH = pl.DeviceIdType.MESH
MIB = 1 << 20


def two_pieces(value):
    high = value.astype(jnp.bfloat16).astype(jnp.float32)
    return jnp.concatenate([high, value - high], axis=0).astype(jnp.bfloat16)


def gather_kernel(index_ref, count_ref, sky_ref, out_ref, column_ref):
    capacity, patches = index_ref.shape
    step = pl.program_id(0)

    @pl.when(step == 0)
    def _():
        slot = lax.broadcasted_iota(jnp.int32, (capacity, patches), 0)
        index = jnp.where(slot < count_ref[...], index_ref[...], -1)
        for d in range(patches):
            column_ref[capacity * d : capacity * (d + 1), :] = jnp.broadcast_to(index[:, d : d + 1], (capacity, 128))

    column = column_ref[pl.ds(pl.multiple_of(step * 128, 128), 128), :]
    lane = lax.broadcasted_iota(jnp.int32, (128, 128), 1)
    pieces = [(column == lane + 128 * t) for t in range(sky_ref.shape[0] // 128)]
    pick = jnp.concatenate([jnp.where(p, 1.0, 0.0) for p in pieces], axis=1).astype(jnp.bfloat16)
    out_ref[...] = jnp.dot(pick, sky_ref[...], preferred_element_type=jnp.float32).astype(jnp.bfloat16)


def gather_rows(index, count, sky):
    slots = index.shape[0] * index.shape[1]
    channels = sky.shape[1]
    whole = lambda a: pl.BlockSpec(a.shape, lambda i: (0, 0))
    return pl.pallas_call(
        gather_kernel,
        grid=(slots // 128,),
        out_shape=jax.ShapeDtypeStruct((slots, channels), jnp.bfloat16),
        in_specs=[whole(index), whole(count), whole(sky)],
        out_specs=pl.BlockSpec((128, channels), lambda i: (i, 0)),
        scratch_shapes=[pltpu.VMEM((slots, 128), jnp.int32)],
        compiler_params=pltpu.CompilerParams(vmem_limit_bytes=24 * MIB),
    )(index, count, sky)


def gram_kernel(x_ref, out_ref):
    width = out_ref.shape[1]
    start = pl.multiple_of(pl.program_id(0) * width, width)
    gram = lax.dot_general(
        x_ref[:, pl.ds(start, width)], x_ref[...], (((0,), (0,)), ((), ())), preferred_element_type=jnp.float32
    )
    high = gram.astype(jnp.bfloat16)
    out_ref[0] = high
    out_ref[1] = (gram - high.astype(jnp.float32)).astype(jnp.bfloat16)


def grams(x):
    rows, channels = x.shape
    width = 256
    return pl.pallas_call(
        gram_kernel,
        grid=(channels // width,),
        out_shape=jax.ShapeDtypeStruct((2, channels, channels), jnp.bfloat16),
        in_specs=[pl.BlockSpec((rows, channels), lambda t: (0, 0))],
        out_specs=pl.BlockSpec((2, width, channels), lambda t: (0, t, 0)),
        compiler_params=pltpu.CompilerParams(vmem_limit_bytes=32 * MIB),
    )(x)


def orthonormal_rows(v):
    row = lax.broadcasted_iota(jnp.int32, (MODES, 1), 0)
    norms = jnp.zeros((MODES, 1), jnp.float32)
    for k in range(MODES):
        lead = v[k : k + 1]
        dots = jnp.sum(v * lead, axis=1, keepdims=True)
        norms = jnp.where(row == k, dots, norms)
        if k + 1 < MODES:
            v = v - jnp.where(row > k, dots / (dots[k : k + 1] + 1e-12), 0.0) * lead
    return v / jnp.sqrt(norms + 1e-12)


def stacked(z, folds):
    width = z.shape[1] // folds
    return jnp.concatenate([z[:, width * f : width * (f + 1)] for f in range(folds)], axis=0)


def unstacked(z, folds):
    return jnp.concatenate([z[MODES * f : MODES * (f + 1)] for f in range(folds)], axis=1)


def sweep_kernel(gram_ref, q0_ref, out_ref, q_ref, exact, short, x_send, x_recv, s_send, s_recv):
    me = lax.axis_index("zp")
    barrier = pltpu.get_barrier_semaphore()
    for o in range(1, SHARERS):
        pl.semaphore_signal(barrier, inc=1, device_id={"zp": lax.rem(me + o, SHARERS)}, device_id_type=MESH)
    pl.semaphore_wait(barrier, SHARERS - 1)

    q_ref[...] = q0_ref[...]

    def partial():
        lhs = two_pieces(q_ref[...])
        z = jnp.dot(jnp.concatenate([lhs, lhs], axis=1), gram_ref[...], preferred_element_type=jnp.float32)
        return z[:MODES] + z[MODES:]

    def exchange(box, send_sem, recv_sem):
        copies = [
            pltpu.make_async_remote_copy(
                src_ref=box.at[me],
                dst_ref=box.at[me],
                send_sem=send_sem.at[o],
                recv_sem=recv_sem.at[o],
                device_id={"zp": lax.rem(me + o, SHARERS)},
                device_id_type=MESH,
            )
            for o in range(1, SHARERS)
        ]
        for each in copies:
            each.start()
        for each in copies:
            each.wait()
        total = box[0].astype(jnp.float32)
        for k in range(1, SHARERS):
            total = total + box[k].astype(jnp.float32)
        return total

    def sweep(step, wide):
        folds, box, sems = (2, exact, (x_send, x_recv)) if wide else (4, short, (s_send, s_recv))
        slot = lax.rem(step, 2)
        box = box.at[slot]
        box[me] = stacked(partial(), folds).astype(box.dtype)
        total = exchange(box, sems[0].at[slot], sems[1].at[slot])
        q_ref[...] = orthonormal_rows(unstacked(total, folds))

    def loop(first, last, wide):
        def body(step, carry):
            sweep(step, wide)
            return carry

        lax.fori_loop(first, last, body, 0)

    loop(0, 2, True)
    loop(2, ITERS - 1, False)
    loop(ITERS - 1, ITERS, True)
    q = q_ref[...]
    channels = q.shape[1]
    q = jnp.concatenate([q, jnp.zeros((PAD - MODES, channels), jnp.float32)], axis=0).astype(jnp.bfloat16)
    out_ref[0] = q[:, : channels // 2]
    out_ref[1] = q[:, channels // 2 :]


def sweeps(gram, q0):
    channels = q0.shape[1]
    vmem = pl.BlockSpec(memory_space=pltpu.VMEM)
    return pl.pallas_call(
        sweep_kernel,
        out_shape=jax.ShapeDtypeStruct((2, PAD, channels // 2), jnp.bfloat16),
        in_specs=[vmem, vmem],
        out_specs=vmem,
        scratch_shapes=[
            pltpu.VMEM((MODES, channels), jnp.float32),
            pltpu.VMEM((2, SHARERS, 2 * MODES, channels // 2), jnp.float32),
            pltpu.VMEM((2, SHARERS, 4 * MODES, channels // 4), jnp.bfloat16),
            pltpu.SemaphoreType.DMA((2, SHARERS)),
            pltpu.SemaphoreType.DMA((2, SHARERS)),
            pltpu.SemaphoreType.DMA((2, SHARERS)),
            pltpu.SemaphoreType.DMA((2, SHARERS)),
        ],
        compiler_params=pltpu.CompilerParams(
            collective_id=0, has_side_effects=True, vmem_limit_bytes=40 * MIB
        ),
    )(gram, q0)


def share_kernel(b_ref, out_ref, a_send, a_recv, r_send, r_recv, s_send, s_recv):
    y, c, x, zl = (lax.axis_index(name) for name in CELL)
    barrier = pltpu.get_barrier_semaphore()
    ring = lambda at, o: lax.rem(at + o, 4)
    for o in range(1, 4):
        pl.semaphore_signal(barrier, inc=1, device_id={"x": ring(x, o)}, device_id_type=MESH)
        pl.semaphore_signal(barrier, inc=1, device_id={"y": ring(y, o)}, device_id_type=MESH)
    pl.semaphore_signal(barrier, inc=1, device_id={"core": 1 - c}, device_id_type=MESH)
    pl.semaphore_signal(barrier, inc=1, device_id={"zl": 1 - zl}, device_id_type=MESH)
    pl.semaphore_wait(barrier, 8)

    def copy(src, dst, sems, at, to):
        return pltpu.make_async_remote_copy(
            src_ref=src, dst_ref=dst, send_sem=sems[0].at[at], recv_sem=sems[1].at[at],
            device_id=to, device_id_type=MESH,
        )

    near, far, across = (a_send, a_recv), (r_send, r_recv), (s_send, s_recv)
    pair = []
    for h in range(2):
        pair.append(copy(b_ref.at[h], out_ref.at[h, y, c, x, zl], near, 6 + h, {"zl": 1 - zl}))
        pair[h].start()
        out_ref[h, y, c, x, zl] = b_ref[h]
    blocks = [out_ref.at[h, y, c, x] for h in range(2)]
    own = [
        [copy(blocks[0], blocks[0], near, o - 1, {"x": ring(x, o)}) for o in range(1, 4)],
        [copy(blocks[1], blocks[1], near, 2 + o, {"y": ring(y, o)}) for o in range(1, 4)],
    ]
    for h in range(2):
        pair[h].wait_recv()
        for each in own[h]:
            each.start()
    lines = [out_ref.at[0, y, c], out_ref.at[1, :, c, x]]
    sibling = {"core": 1 - c}
    started = pair + own[0] + own[1]
    passed = [[], []]
    crossed = []
    for h, axis in ((0, "y"), (1, "x")):
        at = y if h == 0 else x
        for o in range(3):
            own[h][o].wait_recv()
        for o in range(1, 4):
            passed[h].append(copy(lines[h], lines[h], far, 3 * h + o, {axis: ring(at, o)}))
            passed[h][-1].start()
        crossed.append(copy(lines[h], lines[h], across, 4 * h, sibling))
        crossed[-1].start()
    for o in range(1, 4):
        for h in range(2):
            passed[h][o - 1].wait_recv()
            line = out_ref.at[0, ring(y, 4 - o), c] if h == 0 else out_ref.at[1, :, c, ring(x, 4 - o)]
            crossed.append(copy(line, line, across, 4 * h + o, sibling))
            crossed[-1].start()
    for each in crossed:
        each.wait_recv()
    for each in started + passed[0] + passed[1] + crossed:
        each.wait_send()


def share(basis):
    halves, rows, width = basis.shape
    vmem = pl.BlockSpec(memory_space=pltpu.VMEM)
    return pl.pallas_call(
        share_kernel,
        out_shape=jax.ShapeDtypeStruct((halves, 4, 2, 4, 2, rows, width), jnp.bfloat16),
        in_specs=[vmem],
        out_specs=vmem,
        scratch_shapes=[pltpu.SemaphoreType.DMA((8,))] * 6,
        compiler_params=pltpu.CompilerParams(
            collective_id=1, has_side_effects=True, vmem_limit_bytes=24 * MIB
        ),
    )(basis)


def blend_kernel(index_ref, count_ref, taper_ref, sky_ref, basis_ref, out_ref):
    rows = sky_ref.shape[0]
    capacity, patches = index_ref.shape
    halves, columns, width = basis_ref.shape
    slot = lax.broadcasted_iota(jnp.int32, (capacity, patches), 0)
    index = jnp.where(slot < count_ref[...], index_ref[...], -1)
    pixel = pl.program_id(0) * rows + lax.broadcasted_iota(jnp.int32, (rows, patches), 0)
    weights = jnp.zeros((rows, patches), jnp.float32)
    for j in range(capacity):
        weights = weights + jnp.where(index[j : j + 1, :] == pixel, taper_ref[j : j + 1, :], 0.0)
    total = jnp.sum(weights, axis=1, keepdims=True)
    weights = weights / jnp.where(total > 0, total, 1.0)
    high = weights.astype(jnp.bfloat16).astype(jnp.float32)
    pieces = jnp.concatenate([high, weights - high], axis=1).astype(jnp.bfloat16)
    patch = lax.broadcasted_iota(jnp.int32, (2 * patches, columns), 0)
    offset = lax.broadcasted_iota(jnp.int32, (2 * patches, columns), 1) - PAD * jnp.where(
        patch < patches, patch, patch - patches
    )
    spread = jnp.where((offset >= 0) & (offset < PAD), 1.0, 0.0).astype(jnp.bfloat16)
    spread = jnp.dot(pieces, spread, preferred_element_type=jnp.float32)
    coefficients = sum(
        lax.dot_general(
            sky_ref[:, width * h : width * (h + 1)],
            basis_ref[h],
            (((1,), (1,)), ((), ())),
            preferred_element_type=jnp.float32,
        )
        for h in range(halves)
    )
    amounts = two_pieces(spread * coefficients)
    for h in range(halves):
        taken = jnp.dot(amounts, basis_ref[h], preferred_element_type=jnp.float32)
        part = slice(width * h, width * (h + 1))
        out_ref[:, part] = sky_ref[:, part].astype(jnp.float32) - (taken[:rows] + taken[rows:])


def blend(index, count, taper, sky, basis):
    pixels, channels = sky.shape
    rows = 128
    whole = lambda a: pl.BlockSpec(a.shape, lambda i: (0,) * a.ndim)
    return pl.pallas_call(
        blend_kernel,
        grid=(pixels // rows,),
        out_shape=jax.ShapeDtypeStruct((pixels, channels), jnp.float32),
        in_specs=[
            whole(index),
            whole(count),
            whole(taper),
            pl.BlockSpec((rows, channels), lambda i: (i, 0)),
            whole(basis),
        ],
        out_specs=pl.BlockSpec((rows, channels), lambda i: (i, 0)),
        compiler_params=pltpu.CompilerParams(vmem_limit_bytes=32 * MIB),
    )(index, count, taper, sky, basis)


def local(sky, send_index, send_count, taper, start_basis):
    patches, capacity = send_index.shape[2:]
    channels = sky.shape[1]
    index = send_index.reshape(patches, capacity).T
    count = send_count.reshape(1, patches)
    weight = taper.reshape(patches, capacity).T
    outgoing = gather_rows(index, count, sky)
    x = lax.all_to_all(outgoing.reshape(patches, capacity, channels), CELL, 0, 0, tiled=True)
    basis = sweeps(grams(x.reshape(-1, channels)).reshape(2 * channels, channels), start_basis.T)
    bases = share(basis)
    return blend(index, count, weight, sky, bases.reshape(2, patches * PAD, channels // 2))


def solution(mesh):
    fine = Mesh(mesh.devices.reshape(4, SHARERS, 2, 2, 4), ("y", "zp", "zl", "core", "x"))
    patch = ("y", "zp", "zl", "core")
    rows = P((*patch, "x"), None)
    placed = (rows, P(patch, "x", None, None), P(patch, "x", None), P(patch, "x", None, None), P())
    return jax.shard_map(local, mesh=fine, in_specs=placed, out_specs=rows, check_vma=False)
```

time: 1220 us -> 156 us (0.13)
  other arithmetic: 783 us -> 0 us
  waiting for transfers between devices: 175 us -> 0 us
  Pallas kernels: 0 us -> 90.6 us
  between operations: 63.4 us -> 0.11 us
  matrix products: 50.2 us -> 0 us
  blocking collectives: 109 us -> 61.9 us
  local copies, waits for them, and re-layouts: 15.6 us -> 2.62 us
    reduce_sum x144 -> x0, other arithmetic: 490 us -> none  [the longest x102 414 us: orthonormal(): vector = vector - jnp.sum(earlier * vector) * earlier]
    div x5 -> x0, other arithmetic: 205 us -> none  [orthonormal(): vector = vector / jnp.sqrt(jnp.sum(vector * vector) + 1e-12)]
    psum x1 -> x0, waiting for transfers between devices: 94.5 us -> none  [local(): gram_matrix = lax.psum(gram_local, 'grp')]
    pallas_call x0 -> x5, Pallas kernels: none -> 90.6 us  [the longest x1 50.3 us: sweeps(): pl.pallas_call(sweep_kernel, out_shape=jax.ShapeDtypeStruct((2, PAD, chan...]
    all_to_all x1 -> x0, waiting for transfers between devices: 80.6 us -> none  [local(): lax.all_to_all(cleaned.reshape(patch_count, capacity, channels), 'patch',...]
    dot_general x9 -> x0, matrix products: 50.2 us -> none  [the longest x6 34.9 us: local(): subspace = orthonormal(jnp.dot(gram_matrix, subspace, precision=highest))]
    all_to_all x1, blocking collectives: 109 us -> 61.9 us  [local(): lax.all_to_all(outgoing.reshape(patches, capacity, channels), CELL, 0, 0,...]
    another operation x2 -> x0, other arithmetic: 41.5 us -> none
  transfers between devices with their start and end apart: 2 -> 0, of which waited for: 2 -> 0; matrix products, arithmetic and copies ran while one was open for 1% -> 0% of each run, Pallas kernels for 0% -> 0%
where the time goes in v1:
time: 156 us; the launch traced here: 155 us
  Pallas kernels  90.6 us (58%)
  blocking collectives  61.9 us (40%)
  local copies, waits for them, and re-layouts  2.62 us (2%)
    all_to_all x1, blocking collectives, local(): lax.all_to_all(outgoing.reshape(patches, capacity, channels), CELL, 0, 0,...  61.9 us
    pallas_call x1, Pallas kernels, sweeps(): pl.pallas_call(sweep_kernel, out_shape=jax.ShapeDtypeStruct((2, PAD, chan...  50.3 us
    pallas_call x1, Pallas kernels, share(): pl.pallas_call(share_kernel, out_shape=jax.ShapeDtypeStruct((halves, 4, 2...  21.2 us
    pallas_call x1, Pallas kernels, blend(): pl.pallas_call(blend_kernel, grid=(pixels // rows,), out_shape=jax.ShapeD...  8.02 us
    pallas_call x1, Pallas kernels, gather_rows(): pl.pallas_call(gather_kernel, grid=(slots // 128,), out_shape=jax.ShapeDt...  5.56 us
    pallas_call x1, Pallas kernels, grams(): pl.pallas_call(gram_kernel, grid=(channels // width,), out_shape=jax.Shap...  5.56 us

profile of v1, /device:TPU:1, one launch (start us, length us, event | category | flops | bytes accessed | tf_op | source)
XLA Modules:
  0.0 155.2 jit_solution(16418205482188391370)
XLA Ops:
  0.0 0.0 copy-start
  0.0 1.2 copy-done
  1.2 0.0 copy-start.3
  1.2 0.7 copy-done.3
  1.9 0.0 copy-start.6
  1.9 0.7 copy-done.6
  2.6 5.6 %shard_map.55 = bf16[2048,1024]{1,0:T(8,128)(2,1)S(1)} custom-call(s32[32,64]{1,0:T(8,128)S(1)} %bitcast.17, s32[1,64]{1,0:T(1,128)S(1)} %bitcast.20, bf16[512,1024]{1,0:T(8,128)(2,1)S(1)} %copy-done), custom_call_target="tpu_custom_call" | custom-call | tf_op jit(solution)/shard_map/pallas_call | solution.py:44
  8.2 61.9 %all_to_all.5 = bf16[64,32,1024]{2,1,0:T(8,128)(2,1)S(1)} all-to-all(bf16[64,32,1024]{2,1,0:T(8,128)(2,1)S(1)} %bitcast.14), channel_id=1, replica_groups=mesh['y'=4,'zp'=4,'zl'=2,'core'=2,'x'=4] {'y','core','x','zl'}, dimensions={0} | all-to-all | bytes 8388608 | tf_op jit(solution)/shard_map/all_to_all | solution.py:319
  70.0 0.0 copy-start.2
  70.0 5.6 %shard_map.56 = bf16[2,1024,1024]{2,1,0:T(8,128)(2,1)S(1)} custom-call(bf16[2048,1024]{1,0:T(8,128)(2,1)S(1)} %bitcast.12), custom_call_target="tpu_custom_call" | custom-call | tf_op jit(solution)/shard_map/pallas_call | solution.py:69
  75.6 0.0 copy-start.1
  75.6 0.0 copy-start.4
  75.6 0.0 copy-start.5
  75.6 0.0 copy-start.7
  75.7 0.0 copy-done.2
  75.7 50.3 %shard_map.57.b_ref = bf16[2,16,512]{2,1,0:T(8,128)(2,1)S(1)} custom-call(bf16[2048,1024]{1,0:T(8,128)(2,1)S(1)} %bitcast.13, f32[12,1024]{1,0:T(8,128)S(1)} %bitcast.16), custom_call_target="tpu_custom_call" | custom-call | tf_op jit(solution)/shard_map/pallas_call | solution.py:163
  125.9 21.2 %shard_map.58 = bf16[2,4,2,4,2,16,512]{6,5,4,3,2,1,0:T(8,128)(2,1)S(1)} custom-call(bf16[2,16,512]{2,1,0:T(8,128)(2,1)S(1)} %shard_map.57.b_ref), custom_call_target="tpu_custom_call" | custom-call | tf_op jit(solution)/shard_map/pallas_call | solution.py:244
  147.1 0.0 copy-done.1
  147.1 0.0 copy-done.4
  147.1 0.0 copy-done.5
  147.1 0.0 copy-done.7
  147.1 8.0 %shard_map.59 = f32[512,1024]{1,0:T(8,128)} custom-call(s32[32,64]{1,0:T(8,128)S(1)} %bitcast.18, s32[1,64]{1,0:T(1,128)S(1)} %bitcast.21, f32[32,64]{1,0:T(8,128)S(1)} %bitcast.19, bf16[512,1024]{1,0:T(8,128)(2,1)S(1)} %copy-done.1, bf16[2,1024,512]{2,1,0:T(8,128)(2,1)S(1)} %bitcast.15), custom_call_target="tpu_custom_call" | custom-call | tf_op jit(solution)/shard_map/pallas_call | solution.py:296
Async XLA Ops:
  0.0 1.2 copy-start
  1.2 0.7 copy-start.3
  1.9 0.7 copy-start.6
  70.0 5.6 %copy-start.2 = (f32[1024,12]{0,1:T(8,128)S(1)}, f32[1024,12]{0,1:T(8,128)}, u32[]{:S(2)}) copy-start(f32[1024,12]{0,1:T(8,128)} %param.9) | copy-start | bytes 147460
  75.6 71.5 %copy-start.1 = (bf16[512,1024]{1,0:T(8,128)(2,1)S(1)}, bf16[512,1024]{1,0:T(8,128)(2,1)}, u32[]{:S(2)}) copy-start(bf16[512,1024]{1,0:T(8,128)(2,1)} %sky_ref.3) | copy-start | bytes 3145732
  75.6 71.5 %copy-start.4 = (s32[1,1,64,32]{2,3,1,0:T(8,128)S(1)}, s32[1,1,64,32]{2,3,1,0:T(8,128)}, u32[]{:S(2)}) copy-start(s32[1,1,64,32]{2,3,1,0:T(8,128)} %param.6) | copy-start | bytes 24580
  75.6 71.5 %copy-start.5 = (f32[1,1,64,32]{2,3,1,0:T(8,128)S(1)}, f32[1,1,64,32]{2,3,1,0:T(8,128)}, u32[]{:S(2)}) copy-start(f32[1,1,64,32]{2,3,1,0:T(8,128)} %param.8) | copy-start | bytes 24580
  75.6 71.5 %copy-start.7 = (s32[1,1,64]{2,1,0:T(1,128)S(1)}, s32[1,1,64]{2,1,0:T(1,128)}, u32[]{:S(2)}) copy-start(s32[1,1,64]{2,1,0:T(1,128)} %param.7) | copy-start | bytes 772

commit v2 on v1

v2 whole, which is shorter than its diff:
```python
import jax
import jax.numpy as jnp
from jax import lax
from jax.experimental import pallas as pl
from jax.experimental.pallas import tpu as pltpu
from jax.sharding import Mesh, PartitionSpec as P

ITERS = 6
MODES = 12
SHARERS = 4
PAD = 16
CELL = ("y", "core", "x", "zl")
MESH = pl.DeviceIdType.MESH
MIB = 1 << 20


def two_pieces(value):
    high = value.astype(jnp.bfloat16).astype(jnp.float32)
    return jnp.concatenate([high, value - high], axis=0).astype(jnp.bfloat16)


def collect_kernel(
    index_ref, count_ref, taper_ref, sky_ref, gram_ref, weight_ref, column, rows, inbox, total, send_sem, recv_sem
):
    y, c, x, zl = (lax.axis_index(name) for name in CELL)
    capacity, patches = index_ref.shape
    pixels, channels = sky_ref.shape

    def peer(r):
        o = lax.rem(r * 37, patches)
        to = {
            "x": lax.rem(x + lax.rem(o, 4), 4),
            "y": lax.rem(y + lax.rem(lax.div(o, 4), 4), 4),
            "core": lax.rem(c + lax.rem(lax.div(o, 16), 2), 2),
            "zl": lax.rem(zl + lax.div(o, 32), 2),
        }
        return to, ((to["y"] * 2 + to["core"]) * 4 + to["x"]) * 2 + to["zl"]

    def copy(r):
        return pltpu.make_async_remote_copy(
            src_ref=rows.at[r],
            dst_ref=inbox.at[r],
            send_sem=send_sem.at[r],
            recv_sem=recv_sem.at[r],
            device_id=peer(r)[0],
            device_id_type=MESH,
        )

    def each(first, last, step):
        def body(i, carry):
            step(i)
            return carry

        lax.fori_loop(first, last, body, 0)

    barrier = pltpu.get_barrier_semaphore()
    each(1, patches, lambda r: pl.semaphore_signal(barrier, inc=1, device_id=peer(r)[0], device_id_type=MESH))

    slot = lax.broadcasted_iota(jnp.int32, (capacity, patches), 0)
    index = jnp.where(slot < count_ref[...], index_ref[...], -1)
    for d in range(patches):
        column[d] = jnp.broadcast_to(index[:, d : d + 1], (capacity, 128))
    lane = lax.broadcasted_iota(jnp.int32, (4 * capacity, 128), 1)

    def pick(block):
        near = jnp.concatenate([column[peer(4 * block + j)[1]] for j in range(4)], axis=0)
        hot = [jnp.where(near == lane + 128 * t, 1.0, 0.0) for t in range(pixels // 128)]
        hot = jnp.concatenate(hot, axis=1).astype(jnp.bfloat16)
        found = jnp.dot(hot, sky_ref[...], preferred_element_type=jnp.float32).astype(jnp.bfloat16)
        for j in range(4):
            rows[4 * block + j] = found[capacity * j : capacity * (j + 1)]

    pick(0)
    pl.semaphore_wait(barrier, patches - 1)
    for j in range(1, 4):
        copy(j).start()

    def send(block):
        pick(block)
        for j in range(4):
            copy(4 * block + j).start()

    each(1, patches // 4, send)
    inbox[0] = rows[0]

    for part in range(pixels // 128):
        pixel = 128 * part + lax.broadcasted_iota(jnp.int32, (128, patches), 0)
        weights = jnp.zeros((128, patches), jnp.float32)
        for j in range(capacity):
            weights = weights + jnp.where(index[j : j + 1, :] == pixel, taper_ref[j : j + 1, :], 0.0)
        whole = jnp.sum(weights, axis=1, keepdims=True)
        weights = weights / jnp.where(whole > 0, whole, 1.0)
        high = weights.astype(jnp.bfloat16).astype(jnp.float32)
        weight_ref[128 * part : 128 * (part + 1), :] = jnp.concatenate([high, weights - high], axis=1).astype(
            jnp.bfloat16
        )

    total[...] = jnp.zeros_like(total)
    width = 256

    def add(group):
        each(jnp.maximum(8 * group, 1), 8 * group + 8, lambda r: copy(r).wait_recv())
        block = inbox[pl.ds(8 * group, 8)].reshape(8 * capacity, channels)
        for t in range(channels // width):
            part = slice(width * t, width * (t + 1))
            total[part, :] += lax.dot_general(
                block[:, part], block, (((0,), (0,)), ((), ())), preferred_element_type=jnp.float32
            )

    each(0, patches // 8, add)
    for t in range(channels // width):
        part = slice(width * t, width * (t + 1))
        high = total[part, :].astype(jnp.bfloat16)
        gram_ref[part, :] = high
        gram_ref[channels + width * t : channels + width * (t + 1), :] = (
            total[part, :] - high.astype(jnp.float32)
        ).astype(jnp.bfloat16)
    each(1, patches, lambda r: copy(r).wait_send())


def collect(index, count, taper, sky):
    capacity, patches = index.shape
    pixels, channels = sky.shape
    vmem = pl.BlockSpec(memory_space=pltpu.VMEM)
    return pl.pallas_call(
        collect_kernel,
        out_shape=(
            jax.ShapeDtypeStruct((2 * channels, channels), jnp.bfloat16),
            jax.ShapeDtypeStruct((pixels, 2 * patches), jnp.bfloat16),
        ),
        in_specs=[vmem] * 4,
        out_specs=(vmem, vmem),
        scratch_shapes=[
            pltpu.VMEM((patches, capacity, 128), jnp.int32),
            pltpu.VMEM((patches, capacity, channels), jnp.bfloat16),
            pltpu.VMEM((patches, capacity, channels), jnp.bfloat16),
            pltpu.VMEM((channels, channels), jnp.float32),
            pltpu.SemaphoreType.DMA((patches,)),
            pltpu.SemaphoreType.DMA((patches,)),
        ],
        compiler_params=pltpu.CompilerParams(
            collective_id=1, has_side_effects=True, vmem_limit_bytes=40 * MIB
        ),
    )(index, count, taper, sky)


def orthonormal_rows(v):
    row = lax.broadcasted_iota(jnp.int32, (MODES, 1), 0)
    norms = jnp.zeros((MODES, 1), jnp.float32)
    for k in range(MODES):
        lead = v[k : k + 1]
        dots = jnp.sum(v * lead, axis=1, keepdims=True)
        norms = jnp.where(row == k, dots, norms)
        if k + 1 < MODES:
            v = v - jnp.where(row > k, dots / (dots[k : k + 1] + 1e-12), 0.0) * lead
    return v / jnp.sqrt(norms + 1e-12)


def stacked(z, folds):
    width = z.shape[1] // folds
    return jnp.concatenate([z[:, width * f : width * (f + 1)] for f in range(folds)], axis=0)


def unstacked(z, folds):
    return jnp.concatenate([z[MODES * f : MODES * (f + 1)] for f in range(folds)], axis=1)


def sweep_kernel(
    gram_ref, q0_ref, out_ref, q_ref, exact, short,
    x_send, x_recv, s_send, s_recv, n_send, n_recv, f_send, f_recv, c_send, c_recv,
):
    me = lax.axis_index("zp")
    y, c, x, zl = (lax.axis_index(name) for name in CELL)
    barrier = pltpu.get_barrier_semaphore()
    ring = lambda at, o: lax.rem(at + o, 4)
    for o in range(1, 4):
        for to in ({"zp": ring(me, o)}, {"x": ring(x, o)}, {"y": ring(y, o)}):
            pl.semaphore_signal(barrier, inc=1, device_id=to, device_id_type=MESH)
    for to in ({"core": 1 - c}, {"zl": 1 - zl}):
        pl.semaphore_signal(barrier, inc=1, device_id=to, device_id_type=MESH)
    pl.semaphore_wait(barrier, 11)

    q_ref[...] = q0_ref[...]

    def partial():
        lhs = two_pieces(q_ref[...])
        z = jnp.dot(jnp.concatenate([lhs, lhs], axis=1), gram_ref[...], preferred_element_type=jnp.float32)
        return z[:MODES] + z[MODES:]

    def exchange(box, send_sem, recv_sem):
        copies = [
            pltpu.make_async_remote_copy(
                src_ref=box.at[me],
                dst_ref=box.at[me],
                send_sem=send_sem.at[o],
                recv_sem=recv_sem.at[o],
                device_id={"zp": lax.rem(me + o, SHARERS)},
                device_id_type=MESH,
            )
            for o in range(1, SHARERS)
        ]
        for each in copies:
            each.start()
        for each in copies:
            each.wait()
        total = box[0].astype(jnp.float32)
        for k in range(1, SHARERS):
            total = total + box[k].astype(jnp.float32)
        return total

    def sweep(step, wide):
        folds, box, sems = (2, exact, (x_send, x_recv)) if wide else (4, short, (s_send, s_recv))
        slot = lax.rem(step, 2)
        box = box.at[slot]
        box[me] = stacked(partial(), folds).astype(box.dtype)
        total = exchange(box, sems[0].at[slot], sems[1].at[slot])
        q_ref[...] = orthonormal_rows(unstacked(total, folds))

    def loop(first, last, wide):
        def body(step, carry):
            sweep(step, wide)
            return carry

        lax.fori_loop(first, last, body, 0)

    loop(0, 2, True)
    loop(2, ITERS - 1, False)
    loop(ITERS - 1, ITERS, True)
    q = q_ref[...]
    channels = q.shape[1]
    width = channels // 2
    q = jnp.concatenate([q, jnp.zeros((PAD - MODES, channels), jnp.float32)], axis=0).astype(jnp.bfloat16)

    def copy(src, dst, sems, at, to):
        return pltpu.make_async_remote_copy(
            src_ref=src, dst_ref=dst, send_sem=sems[0].at[at], recv_sem=sems[1].at[at],
            device_id=to, device_id_type=MESH,
        )

    near, far, across = (n_send, n_recv), (f_send, f_recv), (c_send, c_recv)
    pair = []
    for h in range(2):
        out_ref[h, y, c, x, zl] = q[:, width * h : width * (h + 1)]
        block = out_ref.at[h, y, c, x, zl]
        pair.append(copy(block, block, near, 6 + h, {"zl": 1 - zl}))
        pair[h].start()
    blocks = [out_ref.at[h, y, c, x] for h in range(2)]
    own = [
        [copy(blocks[0], blocks[0], near, o - 1, {"x": ring(x, o)}) for o in range(1, 4)],
        [copy(blocks[1], blocks[1], near, 2 + o, {"y": ring(y, o)}) for o in range(1, 4)],
    ]
    for h in range(2):
        pair[h].wait_recv()
        for each in own[h]:
            each.start()
    lines = [out_ref.at[0, y, c], out_ref.at[1, :, c, x]]
    sibling = {"core": 1 - c}
    started = pair + own[0] + own[1]
    passed = [[], []]
    crossed = []
    for h, axis in ((0, "y"), (1, "x")):
        at = y if h == 0 else x
        for o in range(3):
            own[h][o].wait_recv()
        for o in range(1, 4):
            passed[h].append(copy(lines[h], lines[h], far, 3 * h + o, {axis: ring(at, o)}))
            passed[h][-1].start()
        crossed.append(copy(lines[h], lines[h], across, 4 * h, sibling))
        crossed[-1].start()
    for o in range(1, 4):
        for h in range(2):
            passed[h][o - 1].wait_recv()
            line = out_ref.at[0, ring(y, 4 - o), c] if h == 0 else out_ref.at[1, :, c, ring(x, 4 - o)]
            crossed.append(copy(line, line, across, 4 * h + o, sibling))
            crossed[-1].start()
    for each in crossed:
        each.wait_recv()
    for each in started + passed[0] + passed[1] + crossed:
        each.wait_send()


def sweeps(gram, q0):
    channels = q0.shape[1]
    vmem = pl.BlockSpec(memory_space=pltpu.VMEM)
    return pl.pallas_call(
        sweep_kernel,
        out_shape=jax.ShapeDtypeStruct((2, 4, 2, 4, 2, PAD, channels // 2), jnp.bfloat16),
        in_specs=[vmem, vmem],
        out_specs=vmem,
        scratch_shapes=[
            pltpu.VMEM((MODES, channels), jnp.float32),
            pltpu.VMEM((2, SHARERS, 2 * MODES, channels // 2), jnp.float32),
            pltpu.VMEM((2, SHARERS, 4 * MODES, channels // 4), jnp.bfloat16),
            *[pltpu.SemaphoreType.DMA((2, SHARERS))] * 4,
            *[pltpu.SemaphoreType.DMA((8,))] * 6,
        ],
        compiler_params=pltpu.CompilerParams(
            collective_id=0, has_side_effects=True, vmem_limit_bytes=40 * MIB
        ),
    )(gram, q0)


def blend_kernel(weight_ref, sky_ref, basis_ref, out_ref):
    rows = sky_ref.shape[0]
    pieces = weight_ref.shape[1]
    halves, columns, width = basis_ref.shape
    patch = lax.rem(lax.broadcasted_iota(jnp.int32, (pieces, columns), 0), pieces // 2)
    spread = patch == lax.div(lax.broadcasted_iota(jnp.int32, (pieces, columns), 1), PAD)
    spread = jnp.where(spread, 1.0, 0.0).astype(jnp.bfloat16)
    spread = jnp.dot(weight_ref[...], spread, preferred_element_type=jnp.float32)
    coefficients = sum(
        lax.dot_general(
            sky_ref[:, width * h : width * (h + 1)],
            basis_ref[h],
            (((1,), (1,)), ((), ())),
            preferred_element_type=jnp.float32,
        )
        for h in range(halves)
    )
    amounts = two_pieces(spread * coefficients)
    for h in range(halves):
        taken = jnp.dot(amounts, basis_ref[h], preferred_element_type=jnp.float32)
        part = slice(width * h, width * (h + 1))
        out_ref[:, part] = sky_ref[:, part].astype(jnp.float32) - (taken[:rows] + taken[rows:])


def blend(weight, sky, basis):
    pixels, channels = sky.shape
    rows = 256
    return pl.pallas_call(
        blend_kernel,
        grid=(pixels // rows,),
        out_shape=jax.ShapeDtypeStruct((pixels, channels), jnp.float32),
        in_specs=[
            pl.BlockSpec((rows, weight.shape[1]), lambda i: (i, 0)),
            pl.BlockSpec((rows, channels), lambda i: (i, 0)),
            pl.BlockSpec(basis.shape, lambda i: (0, 0, 0)),
        ],
        out_specs=pl.BlockSpec((rows, channels), lambda i: (i, 0)),
        compiler_params=pltpu.CompilerParams(vmem_limit_bytes=32 * MIB),
    )(weight, sky, basis)


def local(sky, send_index, send_count, taper, start_basis):
    patches, capacity = send_index.shape[2:]
    channels = sky.shape[1]
    index = send_index.reshape(patches, capacity).T
    count = send_count.reshape(1, patches)
    gram, weight = collect(index, count, taper.reshape(patches, capacity).T, sky)
    bases = sweeps(gram, start_basis.T)
    return blend(weight, sky, bases.reshape(2, patches * PAD, channels // 2))


def solution(mesh):
    fine = Mesh(mesh.devices.reshape(4, SHARERS, 2, 2, 4), ("y", "zp", "zl", "core", "x"))
    patch = ("y", "zp", "zl", "core")
    rows = P((*patch, "x"), None)
    placed = (rows, P(patch, "x", None, None), P(patch, "x", None), P(patch, "x", None, None), P())
    return jax.shard_map(local, mesh=fine, in_specs=placed, out_specs=rows, check_vma=False)
```

time: 156 us -> 146 us (0.936)
  blocking collectives: 61.9 us -> 0 us
  Pallas kernels: 90.6 us -> 141 us
    all_to_all x1 -> x0, blocking collectives: 61.9 us -> none  [local(): lax.all_to_all(outgoing.reshape(patches, capacity, channels), CELL, 0, 0,...]
    pallas_call x4 -> x2, Pallas kernels: 82.5 us -> 136 us  [the longest x1 69.2 us: sweeps(): pl.pallas_call(sweep_kernel, out_shape=jax.ShapeDtypeStruct((2, 4, 2, 4,...]
    pallas_call x1, Pallas kernels: 8.02 us -> 4.84 us  [blend(): pl.pallas_call(blend_kernel, grid=(pixels // rows,), out_shape=jax.ShapeD...]
    unnamed x16 -> x10, local copies, waits for them, and re-layouts: 2.62 us -> 4.15 us
where the time goes in v2:
time: 146 us; the launch traced here: 145 us
  Pallas kernels  141 us (97%)
  local copies, waits for them, and re-layouts  4.15 us (3%)
    pallas_call x1, Pallas kernels, sweeps(): pl.pallas_call(sweep_kernel, out_shape=jax.ShapeDtypeStruct((2, 4, 2, 4,...  69.2 us
    pallas_call x1, Pallas kernels, collect(): pl.pallas_call(collect_kernel, out_shape=(jax.ShapeDtypeStruct((2 * chann...  66.8 us
    pallas_call x1, Pallas kernels, blend(): pl.pallas_call(blend_kernel, grid=(pixels // rows,), out_shape=jax.ShapeD...  4.84 us
    unnamed x10, local copies, waits for them, and re-layouts  4.15 us

profile of v2, /device:TPU:1, one launch (start us, length us, event | category | flops | bytes accessed | tf_op | source)
XLA Modules:
  0.0 145.1 jit_solution(17762281208779376552)
XLA Ops:
  0.0 0.0 copy-start
  0.0 1.2 copy-done
  1.2 0.0 copy-start.2
  1.2 0.7 copy-done.2
  1.9 0.0 copy-start.3
  1.9 0.7 copy-done.3
  2.7 0.0 copy-start.4
  2.7 0.7 copy-done.4
  3.3 66.8 %shard_map.55 = (bf16[2048,1024]{1,0:T(8,128)(2,1)S(1)}, bf16[512,128]{1,0:T(8,128)(2,1)S(1)}) custom-call(s32[32,64]{1,0:T(8,128)S(1)} %bitcast.11, s32[1,64]{1,0:T(1,128)S(1)} %bitcast.13, f32[32,64]{1,0:T(8,128)S(1)} %bitcast.12, bf16[512,1024]{1,0:T(8,128)(2,1)S(1)} %copy-done), custom_call_target="tpu_custom_call" | custom-call | tf_op jit(solution)/shard_map/pallas_call | solution.py:125
  70.2 0.0 copy-start.1
  70.2 0.8 copy-done.1
  71.0 69.2 %shard_map.56 = bf16[2,4,2,4,2,16,512]{6,5,4,3,2,1,0:T(8,128)(2,1)S(1)} custom-call(bf16[2048,1024]{1,0:T(8,128)(2,1)S(1)} %get-tuple-element.8.gram_ref, f32[12,1024]{1,0:T(8,128)S(1)} %bitcast.10), custom_call_target="tpu_custom_call" | custom-call | tf_op jit(solution)/shard_map/pallas_call | solution.py:285
  140.2 4.8 %shard_map.57 = f32[512,1024]{1,0:T(8,128)} custom-call(bf16[512,128]{1,0:T(8,128)(2,1)S(1)} %get-tuple-element.7.weight_ref, bf16[512,1024]{1,0:T(8,128)(2,1)S(1)} %copy-done, bf16[2,1024,512]{2,1,0:T(8,128)(2,1)S(1)} %bitcast.9), custom_call_target="tpu_custom_call" | custom-call | tf_op jit(solution)/shard_map/pallas_call | solution.py:330
Async XLA Ops:
  0.0 1.2 copy-start
  1.2 0.7 copy-start.2
  1.9 0.7 copy-start.3
  2.7 0.7 copy-start.4
  70.2 0.8 copy-start.1

commit v3 on v0

v3 whole, which is shorter than its diff:
```python
import jax
import jax.numpy as jnp
from jax import lax
from jax.experimental import pallas as pl
from jax.experimental.pallas import tpu as pltpu
from jax.sharding import Mesh, PartitionSpec as P

ITERS = 6
MODES = 12
SHARERS = 4
PAD = 16
CELL = ("y", "core", "x", "zl")
MESH = pl.DeviceIdType.MESH
MIB = 1 << 20
VMEM_MIB = 56


def two_pieces(value):
    high = value.astype(jnp.bfloat16).astype(jnp.float32)
    return jnp.concatenate([high, value - high], axis=0).astype(jnp.bfloat16)


def orthonormal_rows(v):
    row = lax.broadcasted_iota(jnp.int32, (MODES, 1), 0)
    norms = jnp.zeros((MODES, 1), jnp.float32)
    for k in range(MODES):
        lead = v[k : k + 1]
        dots = jnp.sum(v * lead, axis=1, keepdims=True)
        norms = jnp.where(row == k, dots, norms)
        if k + 1 < MODES:
            v = v - jnp.where(row > k, dots / (dots[k : k + 1] + 1e-12), 0.0) * lead
    return v / jnp.sqrt(norms + 1e-12)


def stacked(z, folds):
    width = z.shape[1] // folds
    return jnp.concatenate([z[:, width * f : width * (f + 1)] for f in range(folds)], axis=0)


def unstacked(z, folds):
    return jnp.concatenate([z[MODES * f : MODES * (f + 1)] for f in range(folds)], axis=1)


def each(first, last, step):
    def body(i, carry):
        step(i)
        return carry

    lax.fori_loop(first, last, body, 0)


def ring(at, o):
    return lax.rem(at + o, 4)


def send_to(src, dst, send_sem, recv_sem, to):
    return pltpu.make_async_remote_copy(
        src_ref=src, dst_ref=dst, send_sem=send_sem, recv_sem=recv_sem, device_id=to, device_id_type=MESH
    )


def taken_kernel(
    index_hbm, count_hbm, taper_hbm, sky_hbm, q0_hbm, taken_ref,
    index_ref, count_ref, taper_ref, sky_ref, q_ref, bases, weight_ref, column, rows, inbox, total, gram_ref, exact, short,
    in_sem, row_send, row_recv, x_send, x_recv, s_send, s_recv,
    p_send, p_recv, a_send, a_recv, b_send, b_recv, c_send, c_recv,
):
    me = lax.axis_index("zp")
    y, c, x, zl = (lax.axis_index(name) for name in CELL)
    capacity, patches = index_ref.shape
    pixels, channels = sky_ref.shape

    sources = (index_hbm, count_hbm, sky_hbm, taper_hbm, q0_hbm)
    places = (index_ref, count_ref, sky_ref, taper_ref, q_ref)
    loads = [pltpu.make_async_copy(f, t, in_sem.at[i]) for i, (f, t) in enumerate(zip(sources, places))]
    for load in loads:
        load.start()

    def peer(r):
        o = lax.rem(r * 37, patches)
        to = {
            "x": ring(x, lax.rem(o, 4)),
            "y": ring(y, lax.rem(lax.div(o, 4), 4)),
            "core": lax.rem(c + lax.rem(lax.div(o, 16), 2), 2),
            "zl": lax.rem(zl + lax.div(o, 32), 2),
        }
        return to, ((to["y"] * 2 + to["core"]) * 4 + to["x"]) * 2 + to["zl"]

    def row_copy(r):
        return send_to(rows.at[r], inbox.at[r], row_send.at[r], row_recv.at[r], peer(r)[0])

    barrier = pltpu.get_barrier_semaphore()
    each(1, patches, lambda r: pl.semaphore_signal(barrier, inc=1, device_id=peer(r)[0], device_id_type=MESH))
    for o in range(1, SHARERS):
        pl.semaphore_signal(barrier, inc=1, device_id={"zp": ring(me, o)}, device_id_type=MESH)

    loads[0].wait()
    loads[1].wait()
    slot = lax.broadcasted_iota(jnp.int32, (capacity, patches), 0)
    index = jnp.where(slot < count_ref[...], index_ref[...], -1)
    for d in range(patches):
        column[d] = jnp.broadcast_to(index[:, d : d + 1], (capacity, 128))
    lane = lax.broadcasted_iota(jnp.int32, (4 * capacity, 128), 1)
    loads[2].wait()

    def pick(block):
        near = jnp.concatenate([column[peer(4 * block + j)[1]] for j in range(4)], axis=0)
        hot = [jnp.where(near == lane + 128 * t, 1.0, 0.0) for t in range(pixels // 128)]
        hot = jnp.concatenate(hot, axis=1).astype(jnp.bfloat16)
        found = jnp.dot(hot, sky_ref[...], preferred_element_type=jnp.float32).astype(jnp.bfloat16)
        for j in range(4):
            rows[4 * block + j] = found[capacity * j : capacity * (j + 1)]

    pick(0)
    pl.semaphore_wait(barrier, patches - 1 + SHARERS - 1)
    for j in range(1, 4):
        row_copy(j).start()

    def send(block):
        pick(block)
        for j in range(4):
            row_copy(4 * block + j).start()

    each(1, patches // 4, send)
    inbox[0] = rows[0]

    loads[3].wait()
    loads[4].wait()
    for part in range(pixels // 128):
        pixel = 128 * part + lax.broadcasted_iota(jnp.int32, (128, patches), 0)
        weights = jnp.zeros((128, patches), jnp.float32)
        for j in range(capacity):
            weights = weights + jnp.where(index[j : j + 1, :] == pixel, taper_ref[j : j + 1, :], 0.0)
        whole = jnp.sum(weights, axis=1, keepdims=True)
        weights = weights / jnp.where(whole > 0, whole, 1.0)
        high = weights.astype(jnp.bfloat16).astype(jnp.float32)
        weight_ref[128 * part : 128 * (part + 1), :] = jnp.concatenate([high, weights - high], axis=1).astype(
            jnp.bfloat16
        )

    total[...] = jnp.zeros_like(total)
    tile = 256

    def add(group):
        each(jnp.maximum(8 * group, 1), 8 * group + 8, lambda r: row_copy(r).wait_recv())
        block = inbox[pl.ds(8 * group, 8)].reshape(8 * capacity, channels)
        for t in range(channels // tile):
            part = slice(tile * t, tile * (t + 1))
            total[part, :] += lax.dot_general(
                block[:, part], block, (((0,), (0,)), ((), ())), preferred_element_type=jnp.float32
            )

    each(0, patches // 8, add)
    for t in range(channels // tile):
        part = slice(tile * t, tile * (t + 1))
        high = total[part, :].astype(jnp.bfloat16)
        gram_ref[part, :] = high
        gram_ref[channels + tile * t : channels + tile * (t + 1), :] = (
            total[part, :] - high.astype(jnp.float32)
        ).astype(jnp.bfloat16)

    width = channels // 2

    def sweep(step, wide):
        folds, box, sems = (2, exact, (x_send, x_recv)) if wide else (4, short, (s_send, s_recv))
        at = lax.rem(step, 2)
        box = box.at[at]
        lhs = two_pieces(q_ref[...])
        lhs = jnp.concatenate([lhs, lhs], axis=1)
        copies = []
        for h in range(2):
            z = jnp.dot(lhs, gram_ref[:, width * h : width * (h + 1)], preferred_element_type=jnp.float32)
            box[me, h] = stacked(z[:MODES] + z[MODES:], folds).astype(box.dtype)
            for o in (2, 1, 3):
                mine = box.at[me, h]
                copies.append(
                    send_to(mine, mine, sems[0].at[at, 4 * h + o], sems[1].at[at, 4 * h + o], {"zp": ring(me, o)})
                )
                copies[-1].start()
        for one in copies:
            one.wait_recv()
        halves = []
        for h in range(2):
            whole = box[0, h].astype(jnp.float32)
            for k in range(1, SHARERS):
                whole = whole + box[k, h].astype(jnp.float32)
            halves.append(unstacked(whole, folds))
        q_ref[...] = orthonormal_rows(jnp.concatenate(halves, axis=1))
        for one in copies:
            one.wait_send()

    each(0, 2, lambda step: sweep(step, True))
    each(2, ITERS - 1, lambda step: sweep(step, False))
    each(ITERS - 1, ITERS, lambda step: sweep(step, True))

    q = jnp.concatenate([q_ref[...], jnp.zeros((PAD - MODES, channels), jnp.float32)], axis=0)
    q = q.astype(jnp.bfloat16)
    first, second = ("x", "y"), ("y", "x")
    place = {"x": x, "y": y}

    def pair_at(h, i, o):
        back = {first[h]: ring(place[first[h]], 4 - i), second[h]: ring(place[second[h]], 4 - o)}
        return bases.at[h, back["y"], c, back["x"]]

    def line_at(h, o):
        if h == 0:
            return bases.at[0, ring(y, 4 - o), c]
        return bases.at[1, :, c, ring(x, 4 - o)]

    started = []

    def go(src, sems, at, to):
        one = send_to(src, src, sems[0].at[at], sems[1].at[at], to)
        one.start()
        started.append(one)
        return one

    near = [[[None] * 4, [None] * 4] for _ in range(2)]
    far = [[[None] * 4 for _ in range(4)] for _ in range(2)]
    pair = []

    def to_first(h, b):
        block = bases.at[h, y, c, x, zl if b == 0 else 1 - zl]
        for o in (2, 1, 3):
            to = {first[h]: ring(place[first[h]], o)}
            near[h][b][o] = go(block, (a_send, a_recv), 8 * h + 4 * b + o, to)

    def to_second(h, i):
        for o in (2, 1, 3):
            to = {second[h]: ring(place[second[h]], o)}
            far[h][i][o] = go(pair_at(h, i, 0), (b_send, b_recv), 16 * h + 4 * i + o, to)

    def across(h, o):
        return go(line_at(h, o), (c_send, c_recv), 4 * h + o, {"core": 1 - c})

    for h in range(2):
        bases[h, y, c, x, zl] = q[:, width * h : width * (h + 1)]
        pair.append(go(bases.at[h, y, c, x, zl], (p_send, p_recv), h, {"zl": 1 - zl}))
        to_first(h, 0)
    for h in range(2):
        pair[h].wait_recv()
        to_first(h, 1)
        to_second(h, 0)
    for i in (1, 3, 2):
        for h in range(2):
            near[h][0][i].wait_recv()
            near[h][1][i].wait_recv()
            to_second(h, i)
    crossed = [across(0, 0), across(1, 0)]
    for o in (1, 3, 2):
        for h in range(2):
            for i in range(4):
                far[h][i][o].wait_recv()
            crossed.append(across(h, o))
    for one in crossed:
        one.wait_recv()
    for one in started:
        one.wait_send()
    each(1, patches, lambda r: row_copy(r).wait_send())

    columns = patches * PAD
    pieces = 2 * patches
    patch = lax.rem(lax.broadcasted_iota(jnp.int32, (pieces, columns), 0), patches)
    spread = patch == lax.div(lax.broadcasted_iota(jnp.int32, (pieces, columns), 1), PAD)
    spread = jnp.where(spread, 1.0, 0.0).astype(jnp.bfloat16)
    count = 256

    def project(i):
        at = pl.ds(pl.multiple_of(count * i, count), count)
        coefficients = sum(
            lax.dot_general(
                sky_ref[at, width * h : width * (h + 1)],
                bases[h].reshape(columns, width),
                (((1,), (1,)), ((), ())),
                preferred_element_type=jnp.float32,
            )
            for h in range(2)
        )
        amounts = two_pieces(
            jnp.dot(weight_ref[at, :], spread, preferred_element_type=jnp.float32) * coefficients
        )
        for h in range(2):
            taken = jnp.dot(amounts, bases[h].reshape(columns, width), preferred_element_type=jnp.float32)
            taken_ref[at, width * h : width * (h + 1)] = taken[:count] + taken[count:]

    each(0, pixels // count, project)


def taken_from(index, count, taper, sky, q0):
    capacity, patches = index.shape
    pixels, channels = sky.shape
    sems = lambda *shape: pltpu.SemaphoreType.DMA(shape)
    return pl.pallas_call(
        taken_kernel,
        out_shape=jax.ShapeDtypeStruct((pixels, channels), jnp.float32),
        in_specs=[pl.BlockSpec(memory_space=pl.ANY)] * 5,
        out_specs=pl.BlockSpec(memory_space=pltpu.VMEM),
        scratch_shapes=[
            pltpu.VMEM(index.shape, index.dtype),
            pltpu.VMEM(count.shape, count.dtype),
            pltpu.VMEM(taper.shape, taper.dtype),
            pltpu.VMEM(sky.shape, sky.dtype),
            pltpu.VMEM(q0.shape, q0.dtype),
            pltpu.VMEM((2, 4, 2, 4, 2, PAD, channels // 2), jnp.bfloat16),
            pltpu.VMEM((pixels, 2 * patches), jnp.bfloat16),
            pltpu.VMEM((patches, capacity, 128), jnp.int32),
            pltpu.VMEM((patches, capacity, channels), jnp.bfloat16),
            pltpu.VMEM((patches, capacity, channels), jnp.bfloat16),
            pltpu.VMEM((channels, channels), jnp.float32),
            pltpu.VMEM((2 * channels, channels), jnp.bfloat16),
            pltpu.VMEM((2, SHARERS, 2, 2 * MODES, channels // 4), jnp.float32),
            pltpu.VMEM((2, SHARERS, 2, 4 * MODES, channels // 8), jnp.bfloat16),
            sems(5),
            sems(patches), sems(patches),
            sems(2, 8), sems(2, 8), sems(2, 8), sems(2, 8),
            sems(2), sems(2), sems(16), sems(16), sems(32), sems(32), sems(8), sems(8),
        ],
        compiler_params=pltpu.CompilerParams(
            collective_id=0, has_side_effects=True, vmem_limit_bytes=VMEM_MIB * MIB
        ),
    )(index, count, taper, sky, q0)


def local(sky, send_index, send_count, taper, start_basis):
    patches, capacity = send_index.shape[2:]
    index = send_index.reshape(patches, capacity).T
    count = send_count.reshape(1, patches)
    taken = taken_from(index, count, taper.reshape(patches, capacity).T, sky, start_basis.T)
    return sky.astype(jnp.float32) - taken


def solution(mesh):
    fine = Mesh(mesh.devices.reshape(4, SHARERS, 2, 2, 4), ("y", "zp", "zl", "core", "x"))
    patch = ("y", "zp", "zl", "core")
    rows = P((*patch, "x"), None)
    placed = (rows, P(patch, "x", None, None), P(patch, "x", None), P(patch, "x", None, None), P())
    return jax.shard_map(local, mesh=fine, in_specs=placed, out_specs=rows, check_vma=False)
```

time: 1220 us -> 138 us (0.11); the launches traced: 1210 us -> 138 us
  other arithmetic: 783 us -> 3.35 us
  waiting for transfers between devices: 175 us -> 0 us
  Pallas kernels: 0 us -> 135 us
  blocking collectives: 109 us -> 0 us
  between operations: 63.4 us -> 0.02 us
  matrix products: 50.2 us -> 0 us
  local copies, waits for them, and re-layouts: 15.6 us -> 0.01 us
    reduce_sum x144 -> x0, other arithmetic: 490 us -> none  [the longest x102 414 us: orthonormal(): vector = vector - jnp.sum(earlier * vector) * earlier]
    div x5 -> x0, other arithmetic: 205 us -> none  [orthonormal(): vector = vector / jnp.sqrt(jnp.sum(vector * vector) + 1e-12)]
    pallas_call x0 -> x1, Pallas kernels: none -> 135 us  [taken_from(): pl.pallas_call(taken_kernel, out_shape=jax.ShapeDtypeStruct((pixels, chan...]
    all_to_all x1 -> x0, blocking collectives: 109 us -> none  [local(): lax.all_to_all(outgoing, 'patch', split_axis=0, concat_axis=0, tiled=True)]
    psum x1 -> x0, waiting for transfers between devices: 94.5 us -> none  [local(): gram_matrix = lax.psum(gram_local, 'grp')]
    all_to_all x1 -> x0, waiting for transfers between devices: 80.6 us -> none  [local(): lax.all_to_all(cleaned.reshape(patch_count, capacity, channels), 'patch',...]
    dot_general x9 -> x0, matrix products: 50.2 us -> none  [the longest x6 34.9 us: local(): subspace = orthonormal(jnp.dot(gram_matrix, subspace, precision=highest))]
    another operation x2 -> x0, other arithmetic: 41.5 us -> none
  transfers between devices with their start and end apart: 2 -> 0, of which waited for: 2 -> 0; matrix products, arithmetic and copies ran while one was open for 1% -> 0% of each run, Pallas kernels for 0% -> 0%
where the time goes in v3:
time: 138 us
  Pallas kernels  135 us (98%)
  other arithmetic  3.35 us (2%)
    pallas_call x1, Pallas kernels, taken_from(): pl.pallas_call(taken_kernel, out_shape=jax.ShapeDtypeStruct((pixels, chan...  135 us
    sub x1, other arithmetic, local(): return sky.astype(jnp.float32) - taken  3.35 us

profile of v3, /device:TPU:1, one launch (start us, length us, event | category | flops | bytes accessed | tf_op | source)
XLA Modules:
  0.0 137.9 jit_solution(16343469399229095692)
XLA Ops:
  0.0 0.0 copy-start
  0.0 134.6 %shard_map.55 = f32[512,1024]{1,0:T(8,128)} custom-call(s32[32,64]{1,0:T(8,128)} %bitcast.9, s32[1,64]{1,0:T(1,128)} %bitcast.11, f32[32,64]{1,0:T(8,128)} %bitcast.10, bf16[512,1024]{1,0:T(8,128)(2,1)} %sky_hbm.1, f32[12,1024]{1,0:T(8,128)} %bitcast.8), custom_call_target="tpu_custom_call" | custom-call | tf_op jit(solution)/shard_map/pallas_call | solution.py:293
  134.6 0.0 copy-done
  134.6 3.4 %convert_subtract_fusion = f32[512,1024]{1,0:T(8,128)} fusion(f32[512,1024]{1,0:T(8,128)} %shard_map.55, bf16[512,1024]{1,0:T(8,128)(2,1)S(1)} %copy-done), kind=kLoop, calls=%fused_computation | loop fusion | flops 1048576 | bytes 5242880 | tf_op jit(solution)/shard_map/sub | solution.py:329
Async XLA Ops:
  0.0 134.6 %copy-start = (bf16[512,1024]{1,0:T(8,128)(2,1)S(1)}, bf16[512,1024]{1,0:T(8,128)(2,1)}, u32[]{:S(2)}) copy-start(bf16[512,1024]{1,0:T(8,128)(2,1)} %sky_hbm.1) | copy-start | bytes 3145732

commit v4 on v3

--- a/solution.py
+++ b/solution.py
@@ -8,7 +8,6 @@
 ITERS = 6
 MODES = 12
 SHARERS = 4
-PAD = 16
 CELL = ("y", "core", "x", "zl")
 MESH = pl.DeviceIdType.MESH
 MIB = 1 << 20
@@ -59,9 +58,9 @@
     )
 
 
-def taken_kernel(
-    index_hbm, count_hbm, taper_hbm, sky_hbm, q0_hbm, taken_ref,
-    index_ref, count_ref, taper_ref, sky_ref, q_ref, bases, weight_ref, column, rows, inbox, total, gram_ref, exact, short,
+def clean_kernel(
+    index_hbm, count_hbm, taper_hbm, sky_hbm, q0_hbm, clean_ref,
+    index_ref, count_ref, taper_ref, sky_ref, q_ref, duo, bases, basis, weight_ref, column, rows, inbox, total, gram_ref, exact, short,
     in_sem, row_send, row_recv, x_send, x_recv, s_send, s_recv,
     p_send, p_recv, a_send, a_recv, b_send, b_recv, c_send, c_recv,
 ):
@@ -150,26 +149,54 @@
                 block[:, part], block, (((0,), (0,)), ((), ())), preferred_element_type=jnp.float32
             )
 
-    each(0, patches // 8, add)
+    def settle(t, value):
+        high = value.astype(jnp.bfloat16)
+        gram_ref[tile * t : tile * (t + 1), :] = high
+        gram_ref[channels + tile * t : channels + tile * (t + 1), :] = (value - high.astype(jnp.float32)).astype(
+            jnp.bfloat16
+        )
+
+    last = patches // 8 - 1
+    each(0, last, add)
     for t in range(channels // tile):
-        part = slice(tile * t, tile * (t + 1))
-        high = total[part, :].astype(jnp.bfloat16)
-        gram_ref[part, :] = high
-        gram_ref[channels + tile * t : channels + tile * (t + 1), :] = (
-            total[part, :] - high.astype(jnp.float32)
-        ).astype(jnp.bfloat16)
+        settle(t, total[tile * t : tile * (t + 1), :])
+    each(8 * last, patches, lambda r: row_copy(r).wait_recv())
+
+    def late_rows():
+        return inbox[8 * last :].reshape(8 * capacity, channels)
+
+    def settle_late():
+        block = late_rows()
+        for t in range(channels // tile):
+            part = slice(tile * t, tile * (t + 1))
+            settle(
+                t,
+                total[part, :]
+                + lax.dot_general(
+                    block[:, part], block, (((0,), (0,)), ((), ())), preferred_element_type=jnp.float32
+                ),
+            )
 
     width = channels // 2
 
-    def sweep(step, wide):
+    def sweep(step, wide, late=False):
         folds, box, sems = (2, exact, (x_send, x_recv)) if wide else (4, short, (s_send, s_recv))
-        at = lax.rem(step, 2)
+        at = step % 2 if isinstance(step, int) else lax.rem(step, 2)
         box = box.at[at]
-        lhs = two_pieces(q_ref[...])
-        lhs = jnp.concatenate([lhs, lhs], axis=1)
+        pieces = two_pieces(q_ref[...])
+        lhs = jnp.concatenate([pieces, pieces], axis=1)
+        if late:
+            y = lax.dot_general(
+                pieces, late_rows(), (((1,), (1,)), ((), ())), preferred_element_type=jnp.float32
+            )
+            y = two_pieces(y[:MODES] + y[MODES:])
         copies = []
         for h in range(2):
             z = jnp.dot(lhs, gram_ref[:, width * h : width * (h + 1)], preferred_element_type=jnp.float32)
+            if late:
+                z = z + jnp.dot(
+                    y, late_rows()[:, width * h : width * (h + 1)], preferred_element_type=jnp.float32
+                )
             box[me, h] = stacked(z[:MODES] + z[MODES:], folds).astype(box.dtype)
             for o in (2, 1, 3):
                 mine = box.at[me, h]
@@ -177,6 +204,8 @@
                     send_to(mine, mine, sems[0].at[at, 4 * h + o], sems[1].at[at, 4 * h + o], {"zp": ring(me, o)})
                 )
                 copies[-1].start()
+        if late:
+            settle_late()
         for one in copies:
             one.wait_recv()
         halves = []
@@ -189,12 +218,12 @@
         for one in copies:
             one.wait_send()
 
-    each(0, 2, lambda step: sweep(step, True))
-    each(2, ITERS - 1, lambda step: sweep(step, False))
-    each(ITERS - 1, ITERS, lambda step: sweep(step, True))
-
-    q = jnp.concatenate([q_ref[...], jnp.zeros((PAD - MODES, channels), jnp.float32)], axis=0)
-    q = q.astype(jnp.bfloat16)
+    sweep(0, True, late=True)
+    each(1, ITERS - 1, lambda step: sweep(step, False))
+    sweep(ITERS - 1, True)
+
+    blank = jnp.zeros((16 - MODES, channels), jnp.float32)
+    own = jnp.concatenate([q_ref[...], blank], axis=0).astype(jnp.bfloat16)
     first, second = ("x", "y"), ("y", "x")
     place = {"x": x, "y": y}
 
@@ -215,15 +244,14 @@
         started.append(one)
         return one
 
-    near = [[[None] * 4, [None] * 4] for _ in range(2)]
+    near = [[None] * 4 for _ in range(2)]
     far = [[[None] * 4 for _ in range(4)] for _ in range(2)]
     pair = []
 
-    def to_first(h, b):
-        block = bases.at[h, y, c, x, zl if b == 0 else 1 - zl]
+    def to_first(h):
         for o in (2, 1, 3):
             to = {first[h]: ring(place[first[h]], o)}
-            near[h][b][o] = go(block, (a_send, a_recv), 8 * h + 4 * b + o, to)
+            near[h][o] = go(pair_at(h, 0, 0), (a_send, a_recv), 4 * h + o, to)
 
     def to_second(h, i):
         for o in (2, 1, 3):
@@ -234,17 +262,26 @@
         return go(line_at(h, o), (c_send, c_recv), 4 * h + o, {"core": 1 - c})
 
     for h in range(2):
-        bases[h, y, c, x, zl] = q[:, width * h : width * (h + 1)]
-        pair.append(go(bases.at[h, y, c, x, zl], (p_send, p_recv), h, {"zl": 1 - zl}))
-        to_first(h, 0)
+        duo[zl, h] = own[:, width * h : width * (h + 1)]
+        pair.append(go(duo.at[zl, h], (p_send, p_recv), h, {"zl": 1 - zl}))
     for h in range(2):
         pair[h].wait_recv()
-        to_first(h, 1)
+        one, two = (duo[k, h].astype(jnp.float32) for k in range(2))
+        rest = jnp.concatenate([one[8:MODES], two[8:MODES]], axis=0)
+        fold = width // 2
+        block = jnp.concatenate(
+            [
+                jnp.concatenate([one[:8], two[:8]], axis=0),
+                jnp.concatenate([rest[:, :fold], rest[:, fold:]], axis=0),
+            ],
+            axis=1,
+        )
+        bases[h, y, c, x] = block.astype(jnp.bfloat16)
+        to_first(h)
         to_second(h, 0)
     for i in (1, 3, 2):
         for h in range(2):
-            near[h][0][i].wait_recv()
-            near[h][1][i].wait_recv()
+            near[h][i].wait_recv()
             to_second(h, i)
     crossed = [across(0, 0), across(1, 0)]
     for o in (1, 3, 2):
@@ -258,11 +295,19 @@
         one.wait_send()
     each(1, patches, lambda r: row_copy(r).wait_send())
 
-    columns = patches * PAD
+    plain = patches // 2 * 16
+    columns = patches * MODES
+    for h in range(2):
+        block = bases[h].reshape(patches // 2, 16, width + width // 2)
+        basis[h, :plain] = block[:, :, :width].reshape(plain, width)
+        rest = block[:, :, width:].astype(jnp.float32)
+        rest = jnp.concatenate([rest[:, :8], rest[:, 8:]], axis=2)
+        basis[h, plain:] = rest.reshape(columns - plain, width).astype(jnp.bfloat16)
     pieces = 2 * patches
     patch = lax.rem(lax.broadcasted_iota(jnp.int32, (pieces, columns), 0), patches)
-    spread = patch == lax.div(lax.broadcasted_iota(jnp.int32, (pieces, columns), 1), PAD)
-    spread = jnp.where(spread, 1.0, 0.0).astype(jnp.bfloat16)
+    at = lax.broadcasted_iota(jnp.int32, (pieces, columns), 1)
+    owner = jnp.where(at < plain, lax.div(at, 8), lax.div(at - plain, 4))
+    spread = jnp.where(patch == owner, 1.0, 0.0).astype(jnp.bfloat16)
     count = 256
 
     def project(i):
@@ -270,7 +315,7 @@
         coefficients = sum(
             lax.dot_general(
                 sky_ref[at, width * h : width * (h + 1)],
-                bases[h].reshape(columns, width),
+                basis[h],
                 (((1,), (1,)), ((), ())),
                 preferred_element_type=jnp.float32,
             )
@@ -280,18 +325,19 @@
             jnp.dot(weight_ref[at, :], spread, preferred_element_type=jnp.float32) * coefficients
         )
         for h in range(2):
-            taken = jnp.dot(amounts, bases[h].reshape(columns, width), preferred_element_type=jnp.float32)
-            taken_ref[at, width * h : width * (h + 1)] = taken[:count] + taken[count:]
+            taken = jnp.dot(amounts, basis[h], preferred_element_type=jnp.float32)
+            part = slice(width * h, width * (h + 1))
+            clean_ref[at, part] = sky_ref[at, part].astype(jnp.float32) - (taken[:count] + taken[count:])
 
     each(0, pixels // count, project)
 
 
-def taken_from(index, count, taper, sky, q0):
+def cleaned(index, count, taper, sky, q0):
     capacity, patches = index.shape
     pixels, channels = sky.shape
     sems = lambda *shape: pltpu.SemaphoreType.DMA(shape)
     return pl.pallas_call(
-        taken_kernel,
+        clean_kernel,
         out_shape=jax.ShapeDtypeStruct((pixels, channels), jnp.float32),
         in_specs=[pl.BlockSpec(memory_space=pl.ANY)] * 5,
         out_specs=pl.BlockSpec(memory_space=pltpu.VMEM),
@@ -301,7 +347,9 @@
             pltpu.VMEM(taper.shape, taper.dtype),
             pltpu.VMEM(sky.shape, sky.dtype),
             pltpu.VMEM(q0.shape, q0.dtype),
-            pltpu.VMEM((2, 4, 2, 4, 2, PAD, channels // 2), jnp.bfloat16),
+            pltpu.VMEM((2, 2, 16, channels // 2), jnp.bfloat16),
+            pltpu.VMEM((2, 4, 2, 4, 16, channels * 3 // 4), jnp.bfloat16),
+            pltpu.VMEM((2, patches * MODES, channels // 2), jnp.bfloat16),
             pltpu.VMEM((pixels, 2 * patches), jnp.bfloat16),
             pltpu.VMEM((patches, capacity, 128), jnp.int32),
             pltpu.VMEM((patches, capacity, channels), jnp.bfloat16),
@@ -313,7 +361,7 @@
             sems(5),
             sems(patches), sems(patches),
             sems(2, 8), sems(2, 8), sems(2, 8), sems(2, 8),
-            sems(2), sems(2), sems(16), sems(16), sems(32), sems(32), sems(8), sems(8),
+            sems(2), sems(2), sems(8), sems(8), sems(32), sems(32), sems(8), sems(8),
         ],
         compiler_params=pltpu.CompilerParams(
             collective_id=0, has_side_effects=True, vmem_limit_bytes=VMEM_MIB * MIB
@@ -325,8 +373,7 @@
     patches, capacity = send_index.shape[2:]
     index = send_index.reshape(patches, capacity).T
     count = send_count.reshape(1, patches)
-    taken = taken_from(index, count, taper.reshape(patches, capacity).T, sky, start_basis.T)
-    return sky.astype(jnp.float32) - taken
+    return cleaned(index, count, taper.reshape(patches, capacity).T, sky, start_basis.T)
 
 
 def solution(mesh):

time: 138 us -> 134 us (0.971)
  Pallas kernels: 135 us -> 131 us
  other arithmetic: 3.35 us -> 0 us
  local copies, waits for them, and re-layouts: 0.01 us -> 3.16 us
    pallas_call x1, Pallas kernels: 135 us -> 131 us  [cleaned(): pl.pallas_call(clean_kernel, out_shape=jax.ShapeDtypeStruct((pixels, chan...]
    sub x1 -> x0, other arithmetic: 3.35 us -> none  [local(): return sky.astype(jnp.float32) - taken]
    unnamed x2 -> x1, local copies, waits for them, and re-layouts: 0.01 us -> 3.16 us
where the time goes in v4:
time: 134 us
  Pallas kernels  131 us (98%)
  local copies, waits for them, and re-layouts  3.16 us (2%)
    pallas_call x1, Pallas kernels, cleaned(): pl.pallas_call(clean_kernel, out_shape=jax.ShapeDtypeStruct((pixels, chan...  131 us
    unnamed x1, local copies, waits for them, and re-layouts  3.16 us

profile of v4, /device:TPU:1, one launch (start us, length us, event | category | flops | bytes accessed | tf_op | source)
XLA Modules:
  0.0 134.1 jit_solution(10526220162987410596)
XLA Ops:
  0.0 130.9 %shard_map.55 = f32[512,1024]{1,0:T(8,128)} custom-call(s32[32,64]{1,0:T(8,128)} %bitcast.9, s32[1,64]{1,0:T(1,128)} %bitcast.11, f32[32,64]{1,0:T(8,128)} %bitcast.10, bf16[512,1024]{1,0:T(8,128)(2,1)} %sky_hbm.1, f32[12,1024]{1,0:T(8,128)} %bitcast.8), custom_call_target="tpu_custom_call" | custom-call | tf_op jit(solution)/shard_map/pallas_call | solution.py:339
  131.0 3.2 %copy.7 = f32[512,1024]{1,0:T(8,128)} copy(f32[512,1024]{1,0:T(8,128)} %shard_map.55) | data formatting | bytes 4194304

commit v5 on v4

--- a/solution.py
+++ b/solution.py
@@ -12,6 +12,7 @@
 MESH = pl.DeviceIdType.MESH
 MIB = 1 << 20
 VMEM_MIB = 56
+WINDOW = 4
 
 
 def two_pieces(value):
@@ -28,7 +29,25 @@
         norms = jnp.where(row == k, dots, norms)
         if k + 1 < MODES:
             v = v - jnp.where(row > k, dots / (dots[k : k + 1] + 1e-12), 0.0) * lead
-    return v / jnp.sqrt(norms + 1e-12)
+    return v * (1.0 / jnp.sqrt(norms + 1e-12))
+
+
+def orthonormal_pairs(v):
+    row = lax.broadcasted_iota(jnp.int32, (MODES, 1), 0)
+    norms = jnp.ones((MODES, 1), jnp.float32)
+    for k in range(0, MODES, 2):
+        a, b = v[k : k + 1], v[k + 1 : k + 2]
+        on_a = jnp.sum(v * a, axis=1, keepdims=True)
+        on_b = jnp.sum(v * b, axis=1, keepdims=True)
+        aa, ab, bb = on_a[k : k + 1], on_a[k + 1 : k + 2], on_b[k + 1 : k + 2]
+        by_a = on_a / (aa + 1e-12)
+        c = by_a[k + 1 : k + 2]
+        rest = jnp.maximum(bb - 2.0 * c * ab + c * c * aa, 1e-6 * bb)
+        on_rest = on_b - c * on_a - by_a * ab + by_a * (c * aa)
+        by_rest = jnp.where(row > k + 1, on_rest / (rest + 1e-12), 0.0)
+        v = v - (jnp.where(row > k, by_a, 0.0) - by_rest * c) * a - by_rest * b
+        norms = jnp.where(row == k, aa, jnp.where(row == k + 1, rest, norms))
+    return v * (1.0 / jnp.sqrt(norms + 1e-12))
 
 
 def stacked(z, folds):
@@ -59,9 +78,9 @@
 
 
 def clean_kernel(
-    index_hbm, count_hbm, taper_hbm, sky_hbm, q0_hbm, clean_ref,
-    index_ref, count_ref, taper_ref, sky_ref, q_ref, duo, bases, basis, weight_ref, column, rows, inbox, total, gram_ref, exact, short,
-    in_sem, row_send, row_recv, x_send, x_recv, s_send, s_recv,
+    index_hbm, count_hbm, taper_hbm, sky_hbm, q0_hbm, clean_hbm,
+    clean_ref, index_ref, count_ref, taper_ref, sky_ref, q_ref, duo, bases, basis, weight_ref, column, rows, inbox, total, gram_ref, exact, short,
+    in_sem, out_sem, row_send, row_recv, x_send, x_recv, s_send, s_recv,
     p_send, p_recv, a_send, a_recv, b_send, b_recv, c_send, c_recv,
 ):
     me = lax.axis_index("zp")
@@ -89,7 +108,15 @@
         return send_to(rows.at[r], inbox.at[r], row_send.at[r], row_recv.at[r], peer(r)[0])
 
     barrier = pltpu.get_barrier_semaphore()
-    each(1, patches, lambda r: pl.semaphore_signal(barrier, inc=1, device_id=peer(r)[0], device_id_type=MESH))
+    at_x, at_y = [ring(x, o) for o in range(4)], [ring(y, o) for o in range(4)]
+    for o in range(1, patches):
+        to = {
+            "x": at_x[o % 4],
+            "y": at_y[o // 4 % 4],
+            "core": 1 - c if o // 16 % 2 else c,
+            "zl": 1 - zl if o // 32 else zl,
+        }
+        pl.semaphore_signal(barrier, inc=1, device_id=to, device_id_type=MESH)
     for o in range(1, SHARERS):
         pl.semaphore_signal(barrier, inc=1, device_id={"zp": ring(me, o)}, device_id_type=MESH)
 
@@ -120,7 +147,7 @@
         for j in range(4):
             row_copy(4 * block + j).start()
 
-    each(1, patches // 4, send)
+    each(1, WINDOW, send)
     inbox[0] = rows[0]
 
     loads[3].wait()
@@ -157,7 +184,20 @@
         )
 
     last = patches // 8 - 1
-    each(0, last, add)
+
+    def send_on(block):
+        first = 4 * (block - WINDOW)
+        each(jnp.maximum(first, 1), first + 4, lambda r: row_copy(r).wait_send())
+        send(block)
+
+    def send_and_add(group):
+        send_on(2 * group + WINDOW)
+        send_on(2 * group + WINDOW + 1)
+        add(group)
+
+    paired = (patches // 4 - WINDOW) // 2
+    each(0, paired, send_and_add)
+    each(paired, last, add)
     for t in range(channels // tile):
         settle(t, total[tile * t : tile * (t + 1), :])
     each(8 * last, patches, lambda r: row_copy(r).wait_recv())
@@ -179,7 +219,7 @@
 
     width = channels // 2
 
-    def sweep(step, wide, late=False):
+    def sweep(step, wide, late=False, final=False):
         folds, box, sems = (2, exact, (x_send, x_recv)) if wide else (4, short, (s_send, s_recv))
         at = step % 2 if isinstance(step, int) else lax.rem(step, 2)
         box = box.at[at]
@@ -206,6 +246,7 @@
                 copies[-1].start()
         if late:
             settle_late()
+            each(patches - 4 * WINDOW, patches, lambda r: row_copy(r).wait_send())
         for one in copies:
             one.wait_recv()
         halves = []
@@ -214,13 +255,14 @@
             for k in range(1, SHARERS):
                 whole = whole + box[k, h].astype(jnp.float32)
             halves.append(unstacked(whole, folds))
-        q_ref[...] = orthonormal_rows(jnp.concatenate(halves, axis=1))
+        whole = jnp.concatenate(halves, axis=1)
+        q_ref[...] = orthonormal_rows(whole) if final else orthonormal_pairs(whole)
         for one in copies:
             one.wait_send()
 
     sweep(0, True, late=True)
     each(1, ITERS - 1, lambda step: sweep(step, False))
-    sweep(ITERS - 1, True)
+    sweep(ITERS - 1, True, final=True)
 
     blank = jnp.zeros((16 - MODES, channels), jnp.float32)
     own = jnp.concatenate([q_ref[...], blank], axis=0).astype(jnp.bfloat16)
@@ -291,9 +333,6 @@
             crossed.append(across(h, o))
     for one in crossed:
         one.wait_recv()
-    for one in started:
-        one.wait_send()
-    each(1, patches, lambda r: row_copy(r).wait_send())
 
     plain = patches // 2 * 16
     columns = patches * MODES
@@ -311,7 +350,7 @@
     count = 256
 
     def project(i):
-        at = pl.ds(pl.multiple_of(count * i, count), count)
+        at = pl.ds(count * i, count)
         coefficients = sum(
             lax.dot_general(
                 sky_ref[at, width * h : width * (h + 1)],
@@ -329,7 +368,16 @@
             part = slice(width * h, width * (h + 1))
             clean_ref[at, part] = sky_ref[at, part].astype(jnp.float32) - (taken[:count] + taken[count:])
 
-    each(0, pixels // count, project)
+    stores = []
+    for i in range(pixels // count):
+        project(i)
+        at = pl.ds(count * i, count)
+        stores.append(pltpu.make_async_copy(clean_ref.at[at], clean_hbm.at[at], out_sem.at[i]))
+        stores[i].start()
+    for one in started:
+        one.wait_send()
+    for store in stores:
+        store.wait()
 
 
 def cleaned(index, count, taper, sky, q0):
@@ -340,8 +388,9 @@
         clean_kernel,
         out_shape=jax.ShapeDtypeStruct((pixels, channels), jnp.float32),
         in_specs=[pl.BlockSpec(memory_space=pl.ANY)] * 5,
-        out_specs=pl.BlockSpec(memory_space=pltpu.VMEM),
+        out_specs=pl.BlockSpec(memory_space=pl.ANY),
         scratch_shapes=[
+            pltpu.VMEM((pixels, channels), jnp.float32),
             pltpu.VMEM(index.shape, index.dtype),
             pltpu.VMEM(count.shape, count.dtype),
             pltpu.VMEM(taper.shape, taper.dtype),
@@ -359,6 +408,7 @@
             pltpu.VMEM((2, SHARERS, 2, 2 * MODES, channels // 4), jnp.float32),
             pltpu.VMEM((2, SHARERS, 2, 4 * MODES, channels // 8), jnp.bfloat16),
             sems(5),
+            sems(2),
             sems(patches), sems(patches),
             sems(2, 8), sems(2, 8), sems(2, 8), sems(2, 8),
             sems(2), sems(2), sems(8), sems(8), sems(32), sems(32), sems(8), sems(8),
@@ -369,11 +419,42 @@
     )(index, count, taper, sky, q0)
 
 
+def copy_kernel(from_ref, to_ref, held, in_sem, out_sem):
+    chunks = in_sem.shape[0]
+    count = held.shape[0] // chunks
+    parts = [pl.ds(count * i, count) for i in range(chunks)]
+    loads = [pltpu.make_async_copy(from_ref.at[p], held.at[p], in_sem.at[i]) for i, p in enumerate(parts)]
+    stores = [pltpu.make_async_copy(held.at[p], to_ref.at[p], out_sem.at[i]) for i, p in enumerate(parts)]
+    for load in loads:
+        load.start()
+    for load, store in zip(loads, stores):
+        load.wait()
+        store.start()
+    for store in stores:
+        store.wait()
+
+
+def copied(array):
+    anywhere = pl.BlockSpec(memory_space=pl.ANY)
+    return pl.pallas_call(
+        copy_kernel,
+        out_shape=jax.ShapeDtypeStruct(array.shape, array.dtype),
+        in_specs=[anywhere],
+        out_specs=anywhere,
+        scratch_shapes=[
+            pltpu.VMEM(array.shape, array.dtype),
+            pltpu.SemaphoreType.DMA((8,)),
+            pltpu.SemaphoreType.DMA((8,)),
+        ],
+        compiler_params=pltpu.CompilerParams(vmem_limit_bytes=VMEM_MIB * MIB),
+    )(array)
+
+
 def local(sky, send_index, send_count, taper, start_basis):
     patches, capacity = send_index.shape[2:]
     index = send_index.reshape(patches, capacity).T
     count = send_count.reshape(1, patches)
-    return cleaned(index, count, taper.reshape(patches, capacity).T, sky, start_basis.T)
+    return copied(cleaned(index, count, taper.reshape(patches, capacity).T, sky, start_basis.T))
 
 
 def solution(mesh):

time: 134 us -> 128 us (0.955)
  local copies, waits for them, and re-layouts: 3.16 us -> 0 us
  Pallas kernels: 131 us -> 128 us
    pallas_call x1, Pallas kernels: 131 us -> 126 us  [cleaned(): pl.pallas_call(clean_kernel, out_shape=jax.ShapeDtypeStruct((pixels, chan...]
    unnamed x1 -> x0, local copies, waits for them, and re-layouts: 3.16 us -> none
    pallas_call x0 -> x1, Pallas kernels: none -> 2.39 us  [copied(): pl.pallas_call(copy_kernel, out_shape=jax.ShapeDtypeStruct(array.shape, a...]
where the time goes in v5:
time: 128 us
  Pallas kernels  128 us (100%)
    pallas_call x1, Pallas kernels, cleaned(): pl.pallas_call(clean_kernel, out_shape=jax.ShapeDtypeStruct((pixels, chan...  126 us

profile of v5, /device:TPU:1, one launch (start us, length us, event | category | flops | bytes accessed | tf_op | source)
XLA Modules:
  0.0 128.1 jit_solution(4466562152626161468)
XLA Ops:
  0.0 125.7 %shard_map.55.from_ref = f32[512,1024]{1,0:T(8,128)} custom-call(s32[32,64]{1,0:T(8,128)} %bitcast.9, s32[1,64]{1,0:T(1,128)} %bitcast.11, f32[32,64]{1,0:T(8,128)} %bitcast.10, bf16[512,1024]{1,0:T(8,128)(2,1)} %sky_hbm.1, f32[12,1024]{1,0:T(8,128)} %bitcast.8), custom_call_target="tpu_custom_call" | custom-call | tf_op jit(solution)/shard_map/pallas_call | solution.py:387
  125.7 2.4 %shard_map.56 = f32[512,1024]{1,0:T(8,128)} custom-call(f32[512,1024]{1,0:T(8,128)} %shard_map.55.from_ref), custom_call_target="tpu_custom_call" | custom-call | tf_op jit(solution)/shard_map/pallas_call | solution.py:439

commit v6 on v5

--- a/solution.py
+++ b/solution.py
@@ -12,7 +12,7 @@
 MESH = pl.DeviceIdType.MESH
 MIB = 1 << 20
 VMEM_MIB = 56
-WINDOW = 4
+WINDOW = 8
 
 
 def two_pieces(value):
@@ -79,7 +79,7 @@
 
 def clean_kernel(
     index_hbm, count_hbm, taper_hbm, sky_hbm, q0_hbm, clean_hbm,
-    clean_ref, index_ref, count_ref, taper_ref, sky_ref, q_ref, duo, bases, basis, weight_ref, column, rows, inbox, total, gram_ref, exact, short,
+    clean_ref, index_ref, count_ref, taper_ref, sky_ref, q_ref, duo, bases, basis, weight_ref, spread, column, rows, inbox, total, gram_ref, exact, short,
     in_sem, out_sem, row_send, row_recv, x_send, x_recv, s_send, s_recv,
     p_send, p_recv, a_send, a_recv, b_send, b_recv, c_send, c_recv,
 ):
@@ -163,6 +163,18 @@
         weight_ref[128 * part : 128 * (part + 1), :] = jnp.concatenate([high, weights - high], axis=1).astype(
             jnp.bfloat16
         )
+
+    plain = patches // 4 * 16
+    columns = patches // 2 * MODES
+    patch = lax.rem(lax.broadcasted_iota(jnp.int32, (2 * patches, columns), 0), patches)
+    col = lax.broadcasted_iota(jnp.int32, (2 * patches, columns), 1)
+    wide_owner = 16 * lax.div(col, 64) + lax.div(lax.rem(col, 64), 8)
+    thin_owner = 16 * lax.div(col - plain, 32) + lax.div(lax.rem(col - plain, 32), 4)
+    owner = jnp.where(col < plain, wide_owner, thin_owner)
+    cores = (c, 1 - c)
+    for k in range(2):
+        hot = jnp.where(patch == owner + 8 * cores[k], 1.0, 0.0).astype(jnp.bfloat16)
+        spread[k] = jnp.dot(weight_ref[...], hot, preferred_element_type=jnp.float32)
 
     total[...] = jnp.zeros_like(total)
     tile = 256
@@ -331,49 +343,42 @@
             for i in range(4):
                 far[h][i][o].wait_recv()
             crossed.append(across(h, o))
+
+    count = 256
+    stores = []
+
+    def project(k):
+        for h in range(2):
+            block = bases[h, :, cores[k]].reshape(patches // 4, 16, width + width // 2)
+            basis[h, :plain] = block[:, :, :width].reshape(plain, width)
+            rest = block[:, :, width:].astype(jnp.float32)
+            rest = jnp.concatenate([rest[:, :8], rest[:, 8:]], axis=2)
+            basis[h, plain:] = rest.reshape(columns - plain, width).astype(jnp.bfloat16)
+        for i in range(pixels // count):
+            at = pl.ds(count * i, count)
+            coefficients = sum(
+                lax.dot_general(
+                    sky_ref[at, width * h : width * (h + 1)],
+                    basis[h],
+                    (((1,), (1,)), ((), ())),
+                    preferred_element_type=jnp.float32,
+                )
+                for h in range(2)
+            )
+            amounts = two_pieces(spread[k, at] * coefficients)
+            for h in range(2):
+                taken = jnp.dot(amounts, basis[h], preferred_element_type=jnp.float32)
+                part = slice(width * h, width * (h + 1))
+                left = sky_ref[at, part].astype(jnp.float32) if k == 0 else clean_ref[at, part]
+                clean_ref[at, part] = left - (taken[:count] + taken[count:])
+            if k == 1:
+                stores.append(pltpu.make_async_copy(clean_ref.at[at], clean_hbm.at[at], out_sem.at[i]))
+                stores[i].start()
+
+    project(0)
     for one in crossed:
         one.wait_recv()
-
-    plain = patches // 2 * 16
-    columns = patches * MODES
-    for h in range(2):
-        block = bases[h].reshape(patches // 2, 16, width + width // 2)
-        basis[h, :plain] = block[:, :, :width].reshape(plain, width)
-        rest = block[:, :, width:].astype(jnp.float32)
-        rest = jnp.concatenate([rest[:, :8], rest[:, 8:]], axis=2)
-        basis[h, plain:] = rest.reshape(columns - plain, width).astype(jnp.bfloat16)
-    pieces = 2 * patches
-    patch = lax.rem(lax.broadcasted_iota(jnp.int32, (pieces, columns), 0), patches)
-    at = lax.broadcasted_iota(jnp.int32, (pieces, columns), 1)
-    owner = jnp.where(at < plain, lax.div(at, 8), lax.div(at - plain, 4))
-    spread = jnp.where(patch == owner, 1.0, 0.0).astype(jnp.bfloat16)
-    count = 256
-
-    def project(i):
-        at = pl.ds(count * i, count)
-        coefficients = sum(
-            lax.dot_general(
-                sky_ref[at, width * h : width * (h + 1)],
-                basis[h],
-                (((1,), (1,)), ((), ())),
-                preferred_element_type=jnp.float32,
-            )
-            for h in range(2)
-        )
-        amounts = two_pieces(
-            jnp.dot(weight_ref[at, :], spread, preferred_element_type=jnp.float32) * coefficients
-        )
-        for h in range(2):
-            taken = jnp.dot(amounts, basis[h], preferred_element_type=jnp.float32)
-            part = slice(width * h, width * (h + 1))
-            clean_ref[at, part] = sky_ref[at, part].astype(jnp.float32) - (taken[:count] + taken[count:])
-
-    stores = []
-    for i in range(pixels // count):
-        project(i)
-        at = pl.ds(count * i, count)
-        stores.append(pltpu.make_async_copy(clean_ref.at[at], clean_hbm.at[at], out_sem.at[i]))
-        stores[i].start()
+    project(1)
     for one in started:
         one.wait_send()
     for store in stores:
@@ -398,8 +403,9 @@
             pltpu.VMEM(q0.shape, q0.dtype),
             pltpu.VMEM((2, 2, 16, channels // 2), jnp.bfloat16),
             pltpu.VMEM((2, 4, 2, 4, 16, channels * 3 // 4), jnp.bfloat16),
-            pltpu.VMEM((2, patches * MODES, channels // 2), jnp.bfloat16),
+            pltpu.VMEM((2, patches // 2 * MODES, channels // 2), jnp.bfloat16),
             pltpu.VMEM((pixels, 2 * patches), jnp.bfloat16),
+            pltpu.VMEM((2, pixels, patches // 2 * MODES), jnp.float32),
             pltpu.VMEM((patches, capacity, 128), jnp.int32),
             pltpu.VMEM((patches, capacity, channels), jnp.bfloat16),
             pltpu.VMEM((patches, capacity, channels), jnp.bfloat16),

time: 128 us -> 129 us (level)
  no operation moved by 1% of the time
where the time goes in v6:
time: 129 us; the launch traced here: 128 us
  Pallas kernels  128 us (99%)
    pallas_call x1, Pallas kernels, cleaned(): pl.pallas_call(clean_kernel, out_shape=jax.ShapeDtypeStruct((pixels, chan...  126 us

profile of v6, /device:TPU:1, one launch (start us, length us, event | category | flops | bytes accessed | tf_op | source)
XLA Modules:
  0.0 128.4 jit_solution(14014798315275013290)
XLA Ops:
  0.0 126.0 %shard_map.55.from_ref = f32[512,1024]{1,0:T(8,128)} custom-call(s32[32,64]{1,0:T(8,128)} %bitcast.9, s32[1,64]{1,0:T(1,128)} %bitcast.11, f32[32,64]{1,0:T(8,128)} %bitcast.10, bf16[512,1024]{1,0:T(8,128)(2,1)} %sky_hbm.1, f32[12,1024]{1,0:T(8,128)} %bitcast.8), custom_call_target="tpu_custom_call" | custom-call | tf_op jit(solution)/shard_map/pallas_call | solution.py:392
  126.0 2.4 %shard_map.56 = f32[512,1024]{1,0:T(8,128)} custom-call(f32[512,1024]{1,0:T(8,128)} %shard_map.55.from_ref), custom_call_target="tpu_custom_call" | custom-call | tf_op jit(solution)/shard_map/pallas_call | solution.py:445

commit v7 on v6

--- a/solution.py
+++ b/solution.py
@@ -12,7 +12,7 @@
 MESH = pl.DeviceIdType.MESH
 MIB = 1 << 20
 VMEM_MIB = 56
-WINDOW = 8
+WINDOW = 4
 
 
 def two_pieces(value):
@@ -231,12 +231,26 @@
 
     width = channels // 2
 
-    def sweep(step, wide, late=False, final=False):
-        folds, box, sems = (2, exact, (x_send, x_recv)) if wide else (4, short, (s_send, s_recv))
-        at = step % 2 if isinstance(step, int) else lax.rem(step, 2)
-        box = box.at[at]
+    odd = lax.rem(me, 2)
+    started = []
+
+    def product(pieces, h):
+        lhs = jnp.concatenate([pieces, pieces], axis=1)
+        z = jnp.dot(lhs, gram_ref[:, width * h : width * (h + 1)], preferred_element_type=jnp.float32)
+        return z[:MODES] + z[MODES:]
+
+    def swap(at, h, turn, value):
+        box = exact.at[at, h, turn]
+        box[0] = value
+        to = ring(me, 1 + 2 * odd if (h + turn) % 2 == 0 else 3 - 2 * odd)
+        sem = (2 * at + h) * 2 + turn
+        one = send_to(box.at[0], box.at[1], x_send.at[sem], x_recv.at[sem], {"zp": to})
+        one.start()
+        started.append(one)
+        return one
+
+    def exact_sweep(at, late):
         pieces = two_pieces(q_ref[...])
-        lhs = jnp.concatenate([pieces, pieces], axis=1)
         if late:
             y = lax.dot_general(
                 pieces, late_rows(), (((1,), (1,)), ((), ())), preferred_element_type=jnp.float32
@@ -244,21 +258,37 @@
             y = two_pieces(y[:MODES] + y[MODES:])
         copies = []
         for h in range(2):
-            z = jnp.dot(lhs, gram_ref[:, width * h : width * (h + 1)], preferred_element_type=jnp.float32)
+            z = product(pieces, h)
             if late:
-                z = z + jnp.dot(
-                    y, late_rows()[:, width * h : width * (h + 1)], preferred_element_type=jnp.float32
-                )
-            box[me, h] = stacked(z[:MODES] + z[MODES:], folds).astype(box.dtype)
+                part = late_rows()[:, width * h : width * (h + 1)]
+                rest = jnp.dot(y, part, preferred_element_type=jnp.float32)
+                z = z + rest[:MODES] + rest[MODES:]
+            copies.append(swap(at, h, 0, stacked(z, 2)))
+        if late:
+            settle_late()
+            each(patches - 4 * WINDOW, patches, lambda r: row_copy(r).wait_send())
+        for turn in range(2):
+            sums = []
+            for h in range(2):
+                copies[h].wait_recv()
+                sums.append(exact[at, h, turn, 0] + exact[at, h, turn, 1])
+                if turn == 0:
+                    copies[h] = swap(at, h, 1, sums[h])
+        return jnp.concatenate([unstacked(one, 2) for one in sums], axis=1)
+
+    def short_sweep(step):
+        at = lax.rem(step, 2)
+        box = short.at[at]
+        pieces = two_pieces(q_ref[...])
+        copies = []
+        for h in range(2):
+            box[me, h] = stacked(product(pieces, h), 4).astype(box.dtype)
             for o in (2, 1, 3):
                 mine = box.at[me, h]
                 copies.append(
-                    send_to(mine, mine, sems[0].at[at, 4 * h + o], sems[1].at[at, 4 * h + o], {"zp": ring(me, o)})
+                    send_to(mine, mine, s_send.at[at, 4 * h + o], s_recv.at[at, 4 * h + o], {"zp": ring(me, o)})
                 )
                 copies[-1].start()
-        if late:
-            settle_late()
-            each(patches - 4 * WINDOW, patches, lambda r: row_copy(r).wait_send())
         for one in copies:
             one.wait_recv()
         halves = []
@@ -266,15 +296,14 @@
             whole = box[0, h].astype(jnp.float32)
             for k in range(1, SHARERS):
                 whole = whole + box[k, h].astype(jnp.float32)
-            halves.append(unstacked(whole, folds))
-        whole = jnp.concatenate(halves, axis=1)
-        q_ref[...] = orthonormal_rows(whole) if final else orthonormal_pairs(whole)
+            halves.append(unstacked(whole, 4))
+        q_ref[...] = orthonormal_pairs(jnp.concatenate(halves, axis=1))
         for one in copies:
             one.wait_send()
 
-    sweep(0, True, late=True)
-    each(1, ITERS - 1, lambda step: sweep(step, False))
-    sweep(ITERS - 1, True, final=True)
+    q_ref[...] = orthonormal_pairs(exact_sweep(0, True))
+    each(1, ITERS - 1, short_sweep)
+    q_ref[...] = orthonormal_rows(exact_sweep(1, False))
 
     blank = jnp.zeros((16 - MODES, channels), jnp.float32)
     own = jnp.concatenate([q_ref[...], blank], axis=0).astype(jnp.bfloat16)
@@ -289,8 +318,6 @@
         if h == 0:
             return bases.at[0, ring(y, 4 - o), c]
         return bases.at[1, :, c, ring(x, 4 - o)]
-
-    started = []
 
     def go(src, sems, at, to):
         one = send_to(src, src, sems[0].at[at], sems[1].at[at], to)
@@ -411,12 +438,12 @@
             pltpu.VMEM((patches, capacity, channels), jnp.bfloat16),
             pltpu.VMEM((channels, channels), jnp.float32),
             pltpu.VMEM((2 * channels, channels), jnp.bfloat16),
-            pltpu.VMEM((2, SHARERS, 2, 2 * MODES, channels // 4), jnp.float32),
+            pltpu.VMEM((2, 2, 2, 2, 2 * MODES, channels // 4), jnp.float32),
             pltpu.VMEM((2, SHARERS, 2, 4 * MODES, channels // 8), jnp.bfloat16),
             sems(5),
             sems(2),
             sems(patches), sems(patches),
-            sems(2, 8), sems(2, 8), sems(2, 8), sems(2, 8),
+            sems(8), sems(8), sems(2, 8), sems(2, 8),
             sems(2), sems(2), sems(8), sems(8), sems(32), sems(32), sems(8), sems(8),
         ],
         compiler_params=pltpu.CompilerParams(

time: 129 us -> 129 us (level)
  no operation moved by 1% of the time
where the time goes in v7:
time: 129 us
  Pallas kernels  129 us (100%)
    pallas_call x1, Pallas kernels, cleaned(): pl.pallas_call(clean_kernel, out_shape=jax.ShapeDtypeStruct((pixels, chan...  127 us

profile of v7, /device:TPU:1, one launch (start us, length us, event | category | flops | bytes accessed | tf_op | source)
XLA Modules:
  0.0 129.0 jit_solution(17526927569158562756)
XLA Ops:
  0.0 126.6 %shard_map.55.from_ref = f32[512,1024]{1,0:T(8,128)} custom-call(s32[32,64]{1,0:T(8,128)} %bitcast.9, s32[1,64]{1,0:T(1,128)} %bitcast.11, f32[32,64]{1,0:T(8,128)} %bitcast.10, bf16[512,1024]{1,0:T(8,128)(2,1)} %sky_hbm.1, f32[12,1024]{1,0:T(8,128)} %bitcast.8), custom_call_target="tpu_custom_call" | custom-call | tf_op jit(solution)/shard_map/pallas_call | solution.py:419
  126.6 2.4 %shard_map.56 = f32[512,1024]{1,0:T(8,128)} custom-call(f32[512,1024]{1,0:T(8,128)} %shard_map.55.from_ref), custom_call_target="tpu_custom_call" | custom-call | tf_op jit(solution)/shard_map/pallas_call | solution.py:472

commit v8 on v6

--- a/solution.py
+++ b/solution.py
@@ -12,7 +12,7 @@
 MESH = pl.DeviceIdType.MESH
 MIB = 1 << 20
 VMEM_MIB = 56
-WINDOW = 8
+WINDOW = 4
 
 
 def two_pieces(value):
@@ -79,9 +79,9 @@
 
 def clean_kernel(
     index_hbm, count_hbm, taper_hbm, sky_hbm, q0_hbm, clean_hbm,
-    clean_ref, index_ref, count_ref, taper_ref, sky_ref, q_ref, duo, bases, basis, weight_ref, spread, column, rows, inbox, total, gram_ref, exact, short,
+    clean_ref, index_ref, count_ref, taper_ref, sky_ref, q_ref, bases, basis, weight_ref, spread, column, rows, inbox, total, gram_ref, exact, short,
     in_sem, out_sem, row_send, row_recv, x_send, x_recv, s_send, s_recv,
-    p_send, p_recv, a_send, a_recv, b_send, b_recv, c_send, c_recv,
+    a_send, a_recv, b_send, b_recv, c_send, c_recv,
 ):
     me = lax.axis_index("zp")
     y, c, x, zl = (lax.axis_index(name) for name in CELL)
@@ -276,14 +276,23 @@
     each(1, ITERS - 1, lambda step: sweep(step, False))
     sweep(ITERS - 1, True, final=True)
 
-    blank = jnp.zeros((16 - MODES, channels), jnp.float32)
-    own = jnp.concatenate([q_ref[...], blank], axis=0).astype(jnp.bfloat16)
+    fold, thin = width // 2, width // 4
     first, second = ("x", "y"), ("y", "x")
     place = {"x": x, "y": y}
 
     def pair_at(h, i, o):
         back = {first[h]: ring(place[first[h]], 4 - i), second[h]: ring(place[second[h]], 4 - o)}
         return bases.at[h, back["y"], c, back["x"]]
+
+    def block_of(q):
+        wide, rest = q[:8], q[8:]
+        return jnp.concatenate(
+            [
+                jnp.concatenate([wide[:, :fold], wide[:, fold:]], axis=0),
+                jnp.concatenate([rest[:, thin * j : thin * (j + 1)] for j in range(4)], axis=0),
+            ],
+            axis=1,
+        )
 
     def line_at(h, o):
         if h == 0:
@@ -298,14 +307,16 @@
         started.append(one)
         return one
 
-    near = [[None] * 4 for _ in range(2)]
+    near = [[[None] * 2 for _ in range(4)] for _ in range(2)]
     far = [[[None] * 4 for _ in range(4)] for _ in range(2)]
-    pair = []
 
     def to_first(h):
-        for o in (2, 1, 3):
-            to = {first[h]: ring(place[first[h]], o)}
-            near[h][o] = go(pair_at(h, 0, 0), (a_send, a_recv), 4 * h + o, to)
+        mine = bases.at[h, y, c, x, zl]
+        for o in (2, 1, 3, 0):
+            for j in range(2):
+                if o + j:
+                    to = {first[h]: ring(place[first[h]], o), "zl": 1 - zl if j else zl}
+                    near[h][o][j] = go(mine, (a_send, a_recv), 8 * h + 2 * o + j, to)
 
     def to_second(h, i):
         for o in (2, 1, 3):
@@ -316,26 +327,13 @@
         return go(line_at(h, o), (c_send, c_recv), 4 * h + o, {"core": 1 - c})
 
     for h in range(2):
-        duo[zl, h] = own[:, width * h : width * (h + 1)]
-        pair.append(go(duo.at[zl, h], (p_send, p_recv), h, {"zl": 1 - zl}))
-    for h in range(2):
-        pair[h].wait_recv()
-        one, two = (duo[k, h].astype(jnp.float32) for k in range(2))
-        rest = jnp.concatenate([one[8:MODES], two[8:MODES]], axis=0)
-        fold = width // 2
-        block = jnp.concatenate(
-            [
-                jnp.concatenate([one[:8], two[:8]], axis=0),
-                jnp.concatenate([rest[:, :fold], rest[:, fold:]], axis=0),
-            ],
-            axis=1,
-        )
-        bases[h, y, c, x] = block.astype(jnp.bfloat16)
+        bases[h, y, c, x, zl] = block_of(q_ref[:, width * h : width * (h + 1)]).astype(jnp.bfloat16)
         to_first(h)
-        to_second(h, 0)
-    for i in (1, 3, 2):
+    for i in (0, 1, 3, 2):
         for h in range(2):
-            near[h][i].wait_recv()
+            for j in range(2):
+                if i + j:
+                    near[h][i][j].wait_recv()
             to_second(h, i)
     crossed = [across(0, 0), across(1, 0)]
     for o in (1, 3, 2):
@@ -349,10 +347,15 @@
 
     def project(k):
         for h in range(2):
-            block = bases[h, :, cores[k]].reshape(patches // 4, 16, width + width // 2)
-            basis[h, :plain] = block[:, :, :width].reshape(plain, width)
-            rest = block[:, :, width:].astype(jnp.float32)
-            rest = jnp.concatenate([rest[:, :8], rest[:, 8:]], axis=2)
+            block = bases[h, :, cores[k]].reshape(patches // 4, 2, 16, fold + thin)
+            wide = block[:, :, :, :fold].astype(jnp.float32)
+            wide = jnp.concatenate([wide[:, :, :8], wide[:, :, 8:]], axis=3)
+            basis[h, :plain] = wide.reshape(plain, width).astype(jnp.bfloat16)
+            rest = block[:, :, :, fold:].astype(jnp.float32)
+            rest = [
+                jnp.concatenate([rest[:, z, 4 * j : 4 * j + 4] for z in range(2)], axis=1) for j in range(4)
+            ]
+            rest = jnp.concatenate(rest, axis=2)
             basis[h, plain:] = rest.reshape(columns - plain, width).astype(jnp.bfloat16)
         for i in range(pixels // count):
             at = pl.ds(count * i, count)
@@ -401,8 +404,7 @@
             pltpu.VMEM(taper.shape, taper.dtype),
             pltpu.VMEM(sky.shape, sky.dtype),
             pltpu.VMEM(q0.shape, q0.dtype),
-            pltpu.VMEM((2, 2, 16, channels // 2), jnp.bfloat16),
-            pltpu.VMEM((2, 4, 2, 4, 16, channels * 3 // 4), jnp.bfloat16),
+            pltpu.VMEM((2, 4, 2, 4, 2, 16, channels * 3 // 8), jnp.bfloat16),
             pltpu.VMEM((2, patches // 2 * MODES, channels // 2), jnp.bfloat16),
             pltpu.VMEM((pixels, 2 * patches), jnp.bfloat16),
             pltpu.VMEM((2, pixels, patches // 2 * MODES), jnp.float32),
@@ -417,7 +419,7 @@
             sems(2),
             sems(patches), sems(patches),
             sems(2, 8), sems(2, 8), sems(2, 8), sems(2, 8),
-            sems(2), sems(2), sems(8), sems(8), sems(32), sems(32), sems(8), sems(8),
+            sems(16), sems(16), sems(32), sems(32), sems(8), sems(8),
         ],
         compiler_params=pltpu.CompilerParams(
             collective_id=0, has_side_effects=True, vmem_limit_bytes=VMEM_MIB * MIB

time: 129 us -> 126 us (0.977)
  Pallas kernels: 128 us -> 126 us
    pallas_call x1, Pallas kernels: 126 us -> 124 us  [cleaned(): pl.pallas_call(clean_kernel, out_shape=jax.ShapeDtypeStruct((pixels, chan...]
where the time goes in v8:
time: 126 us
  Pallas kernels  126 us (100%)
    pallas_call x1, Pallas kernels, cleaned(): pl.pallas_call(clean_kernel, out_shape=jax.ShapeDtypeStruct((pixels, chan...  124 us

profile of v8, /device:TPU:1, one launch (start us, length us, event | category | flops | bytes accessed | tf_op | source)
XLA Modules:
  0.0 126.3 jit_solution(2303042472523796429)
XLA Ops:
  0.0 123.9 %shard_map.55.from_ref = f32[512,1024]{1,0:T(8,128)} custom-call(s32[32,64]{1,0:T(8,128)} %bitcast.9, s32[1,64]{1,0:T(1,128)} %bitcast.11, f32[32,64]{1,0:T(8,128)} %bitcast.10, bf16[512,1024]{1,0:T(8,128)(2,1)} %sky_hbm.1, f32[12,1024]{1,0:T(8,128)} %bitcast.8), custom_call_target="tpu_custom_call" | custom-call | tf_op jit(solution)/shard_map/pallas_call | solution.py:395
  123.9 2.4 %shard_map.56 = f32[512,1024]{1,0:T(8,128)} custom-call(f32[512,1024]{1,0:T(8,128)} %shard_map.55.from_ref), custom_call_target="tpu_custom_call" | custom-call | tf_op jit(solution)/shard_map/pallas_call | solution.py:447

commit v9 on v8

--- a/solution.py
+++ b/solution.py
@@ -12,7 +12,7 @@
 MESH = pl.DeviceIdType.MESH
 MIB = 1 << 20
 VMEM_MIB = 56
-WINDOW = 4
+WINDOW = 2
 
 
 def two_pieces(value):

time: 126 us -> 129 us (1.024)
  Pallas kernels: 126 us -> 129 us
    pallas_call x1, Pallas kernels: 124 us -> 127 us  [cleaned(): pl.pallas_call(clean_kernel, out_shape=jax.ShapeDtypeStruct((pixels, chan...]
where the time goes in v9:
time: 129 us
  Pallas kernels  129 us (100%)
    pallas_call x1, Pallas kernels, cleaned(): pl.pallas_call(clean_kernel, out_shape=jax.ShapeDtypeStruct((pixels, chan...  127 us

profile of v9, /device:TPU:1, one launch (start us, length us, event | category | flops | bytes accessed | tf_op | source)
XLA Modules:
  0.0 129.0 jit_solution(11277831213739887738)
XLA Ops:
  0.0 126.6 %shard_map.55.from_ref = f32[512,1024]{1,0:T(8,128)} custom-call(s32[32,64]{1,0:T(8,128)} %bitcast.9, s32[1,64]{1,0:T(1,128)} %bitcast.11, f32[32,64]{1,0:T(8,128)} %bitcast.10, bf16[512,1024]{1,0:T(8,128)(2,1)} %sky_hbm.1, f32[12,1024]{1,0:T(8,128)} %bitcast.8), custom_call_target="tpu_custom_call" | custom-call | tf_op jit(solution)/shard_map/pallas_call | solution.py:395
  126.6 2.4 %shard_map.56 = f32[512,1024]{1,0:T(8,128)} custom-call(f32[512,1024]{1,0:T(8,128)} %shard_map.55.from_ref), custom_call_target="tpu_custom_call" | custom-call | tf_op jit(solution)/shard_map/pallas_call | solution.py:447

commit v10 on v8

--- a/solution.py
+++ b/solution.py
@@ -21,18 +21,6 @@
 
 
 def orthonormal_rows(v):
-    row = lax.broadcasted_iota(jnp.int32, (MODES, 1), 0)
-    norms = jnp.zeros((MODES, 1), jnp.float32)
-    for k in range(MODES):
-        lead = v[k : k + 1]
-        dots = jnp.sum(v * lead, axis=1, keepdims=True)
-        norms = jnp.where(row == k, dots, norms)
-        if k + 1 < MODES:
-            v = v - jnp.where(row > k, dots / (dots[k : k + 1] + 1e-12), 0.0) * lead
-    return v * (1.0 / jnp.sqrt(norms + 1e-12))
-
-
-def orthonormal_pairs(v):
     row = lax.broadcasted_iota(jnp.int32, (MODES, 1), 0)
     norms = jnp.ones((MODES, 1), jnp.float32)
     for k in range(0, MODES, 2):
@@ -195,7 +183,7 @@
             jnp.bfloat16
         )
 
-    last = patches // 8 - 1
+    last = patches // 8 - 2
 
     def send_on(block):
         first = 4 * (block - WINDOW)
@@ -215,7 +203,7 @@
     each(8 * last, patches, lambda r: row_copy(r).wait_recv())
 
     def late_rows():
-        return inbox[8 * last :].reshape(8 * capacity, channels)
+        return inbox[8 * last :].reshape((patches - 8 * last) * capacity, channels)
 
     def settle_late():
         block = late_rows()
@@ -231,7 +219,7 @@
 
     width = channels // 2
 
-    def sweep(step, wide, late=False, final=False):
+    def sweep(step, wide, late=False):
         folds, box, sems = (2, exact, (x_send, x_recv)) if wide else (4, short, (s_send, s_recv))
         at = step % 2 if isinstance(step, int) else lax.rem(step, 2)
         box = box.at[at]
@@ -259,22 +247,22 @@
         if late:
             settle_late()
             each(patches - 4 * WINDOW, patches, lambda r: row_copy(r).wait_send())
-        for one in copies:
-            one.wait_recv()
         halves = []
         for h in range(2):
+            for one in copies[3 * h : 3 * h + 3]:
+                one.wait_recv()
             whole = box[0, h].astype(jnp.float32)
             for k in range(1, SHARERS):
                 whole = whole + box[k, h].astype(jnp.float32)
             halves.append(unstacked(whole, folds))
         whole = jnp.concatenate(halves, axis=1)
-        q_ref[...] = orthonormal_rows(whole) if final else orthonormal_pairs(whole)
+        q_ref[...] = orthonormal_rows(whole)
         for one in copies:
             one.wait_send()
 
     sweep(0, True, late=True)
     each(1, ITERS - 1, lambda step: sweep(step, False))
-    sweep(ITERS - 1, True, final=True)
+    sweep(ITERS - 1, True)
 
     fold, thin = width // 2, width // 4
     first, second = ("x", "y"), ("y", "x")
@@ -342,7 +330,6 @@
                 far[h][i][o].wait_recv()
             crossed.append(across(h, o))
 
-    count = 256
     stores = []
 
     def project(k):
@@ -357,26 +344,24 @@
             ]
             rest = jnp.concatenate(rest, axis=2)
             basis[h, plain:] = rest.reshape(columns - plain, width).astype(jnp.bfloat16)
-        for i in range(pixels // count):
-            at = pl.ds(count * i, count)
-            coefficients = sum(
-                lax.dot_general(
-                    sky_ref[at, width * h : width * (h + 1)],
-                    basis[h],
-                    (((1,), (1,)), ((), ())),
-                    preferred_element_type=jnp.float32,
-                )
-                for h in range(2)
+        coefficients = sum(
+            lax.dot_general(
+                sky_ref[:, width * h : width * (h + 1)],
+                basis[h],
+                (((1,), (1,)), ((), ())),
+                preferred_element_type=jnp.float32,
             )
-            amounts = two_pieces(spread[k, at] * coefficients)
-            for h in range(2):
-                taken = jnp.dot(amounts, basis[h], preferred_element_type=jnp.float32)
-                part = slice(width * h, width * (h + 1))
-                left = sky_ref[at, part].astype(jnp.float32) if k == 0 else clean_ref[at, part]
-                clean_ref[at, part] = left - (taken[:count] + taken[count:])
+            for h in range(2)
+        )
+        amounts = two_pieces(spread[k] * coefficients)
+        for h in range(2):
+            taken = jnp.dot(amounts, basis[h], preferred_element_type=jnp.float32)
+            part = slice(width * h, width * (h + 1))
+            left = sky_ref[:, part].astype(jnp.float32) if k == 0 else clean_ref[:, part]
+            clean_ref[:, part] = left - (taken[:pixels] + taken[pixels:])
             if k == 1:
-                stores.append(pltpu.make_async_copy(clean_ref.at[at], clean_hbm.at[at], out_sem.at[i]))
-                stores[i].start()
+                stores.append(pltpu.make_async_copy(clean_ref.at[:, part], clean_hbm.at[:, part], out_sem.at[h]))
+                stores[h].start()
 
     project(0)
     for one in crossed:

time: 126 us -> 125 us (level)
  no operation moved by 1% of the time
where the time goes in v10:
time: 125 us
  Pallas kernels  125 us (100%)
    pallas_call x1, Pallas kernels, cleaned(): pl.pallas_call(clean_kernel, out_shape=jax.ShapeDtypeStruct((pixels, chan...  123 us

profile of v10, /device:TPU:1, one launch (start us, length us, event | category | flops | bytes accessed | tf_op | source)
XLA Modules:
  0.0 125.3 jit_solution(11506196825546729137)
XLA Ops:
  0.0 122.9 %shard_map.55.from_ref = f32[512,1024]{1,0:T(8,128)} custom-call(s32[32,64]{1,0:T(8,128)} %bitcast.9, s32[1,64]{1,0:T(1,128)} %bitcast.11, f32[32,64]{1,0:T(8,128)} %bitcast.10, bf16[512,1024]{1,0:T(8,128)(2,1)} %sky_hbm.1, f32[12,1024]{1,0:T(8,128)} %bitcast.8), custom_call_target="tpu_custom_call" | custom-call | tf_op jit(solution)/shard_map/pallas_call | solution.py:380
  122.9 2.4 %shard_map.56 = f32[512,1024]{1,0:T(8,128)} custom-call(f32[512,1024]{1,0:T(8,128)} %shard_map.55.from_ref), custom_call_target="tpu_custom_call" | custom-call | tf_op jit(solution)/shard_map/pallas_call | solution.py:432

commit v11 on v10

--- a/solution.py
+++ b/solution.py
@@ -21,6 +21,18 @@
 
 
 def orthonormal_rows(v):
+    row = lax.broadcasted_iota(jnp.int32, (MODES, 1), 0)
+    norms = jnp.zeros((MODES, 1), jnp.float32)
+    for k in range(MODES):
+        lead = v[k : k + 1]
+        dots = jnp.sum(v * lead, axis=1, keepdims=True)
+        norms = jnp.where(row == k, dots, norms)
+        if k + 1 < MODES:
+            v = v - jnp.where(row > k, dots / (dots[k : k + 1] + 1e-12), 0.0) * lead
+    return v * (1.0 / jnp.sqrt(norms + 1e-12))
+
+
+def orthonormal_pairs(v):
     row = lax.broadcasted_iota(jnp.int32, (MODES, 1), 0)
     norms = jnp.ones((MODES, 1), jnp.float32)
     for k in range(0, MODES, 2):
@@ -97,16 +109,20 @@
 
     barrier = pltpu.get_barrier_semaphore()
     at_x, at_y = [ring(x, o) for o in range(4)], [ring(y, o) for o in range(4)]
-    for o in range(1, patches):
-        to = {
-            "x": at_x[o % 4],
-            "y": at_y[o // 4 % 4],
-            "core": 1 - c if o // 16 % 2 else c,
-            "zl": 1 - zl if o // 32 else zl,
-        }
+    steps = (0, 1, 2, 1)
+    greeted = [(-steps[o % 4] - steps[o // 4 % 4] - o // 32, o) for o in range(1, patches)]
+    greeted += [(-2 * steps[o], -o) for o in range(1, SHARERS)]
+    for _, o in sorted(greeted):
+        if o < 0:
+            to = {"zp": ring(me, -o)}
+        else:
+            to = {
+                "x": at_x[o % 4],
+                "y": at_y[o // 4 % 4],
+                "core": 1 - c if o // 16 % 2 else c,
+                "zl": 1 - zl if o // 32 else zl,
+            }
         pl.semaphore_signal(barrier, inc=1, device_id=to, device_id_type=MESH)
-    for o in range(1, SHARERS):
-        pl.semaphore_signal(barrier, inc=1, device_id={"zp": ring(me, o)}, device_id_type=MESH)
 
     loads[0].wait()
     loads[1].wait()
@@ -219,7 +235,7 @@
 
     width = channels // 2
 
-    def sweep(step, wide, late=False):
+    def sweep(step, wide, late=False, final=False):
         folds, box, sems = (2, exact, (x_send, x_recv)) if wide else (4, short, (s_send, s_recv))
         at = step % 2 if isinstance(step, int) else lax.rem(step, 2)
         box = box.at[at]
@@ -250,19 +266,17 @@
         halves = []
         for h in range(2):
             for one in copies[3 * h : 3 * h + 3]:
-                one.wait_recv()
+                one.wait()
             whole = box[0, h].astype(jnp.float32)
             for k in range(1, SHARERS):
                 whole = whole + box[k, h].astype(jnp.float32)
             halves.append(unstacked(whole, folds))
         whole = jnp.concatenate(halves, axis=1)
-        q_ref[...] = orthonormal_rows(whole)
-        for one in copies:
-            one.wait_send()
+        q_ref[...] = orthonormal_rows(whole) if final else orthonormal_pairs(whole)
 
     sweep(0, True, late=True)
     each(1, ITERS - 1, lambda step: sweep(step, False))
-    sweep(ITERS - 1, True)
+    sweep(ITERS - 1, True, final=True)
 
     fold, thin = width // 2, width // 4
     first, second = ("x", "y"), ("y", "x")

time: 125 us -> 125 us (level)
  no operation moved by 1% of the time
where the time goes in v11:
time: 125 us
  Pallas kernels  125 us (100%)
    pallas_call x1, Pallas kernels, cleaned(): pl.pallas_call(clean_kernel, out_shape=jax.ShapeDtypeStruct((pixels, chan...  123 us

profile of v11, /device:TPU:1, one launch (start us, length us, event | category | flops | bytes accessed | tf_op | source)
XLA Modules:
  0.0 125.3 jit_solution(18439015453309691747)
XLA Ops:
  0.0 122.9 %shard_map.55.from_ref = f32[512,1024]{1,0:T(8,128)} custom-call(s32[32,64]{1,0:T(8,128)} %bitcast.9, s32[1,64]{1,0:T(1,128)} %bitcast.11, f32[32,64]{1,0:T(8,128)} %bitcast.10, bf16[512,1024]{1,0:T(8,128)(2,1)} %sky_hbm.1, f32[12,1024]{1,0:T(8,128)} %bitcast.8), custom_call_target="tpu_custom_call" | custom-call | tf_op jit(solution)/shard_map/pallas_call | solution.py:394
  122.9 2.4 %shard_map.56 = f32[512,1024]{1,0:T(8,128)} custom-call(f32[512,1024]{1,0:T(8,128)} %shard_map.55.from_ref), custom_call_target="tpu_custom_call" | custom-call | tf_op jit(solution)/shard_map/pallas_call | solution.py:446

commit v12 on v11

--- a/solution.py
+++ b/solution.py
@@ -202,18 +202,25 @@
     last = patches // 8 - 2
 
     def send_on(block):
-        first = 4 * (block - WINDOW)
-        each(jnp.maximum(first, 1), first + 4, lambda r: row_copy(r).wait_send())
-        send(block)
+        pick(block)
+        for j in range(4):
+            row_copy(4 * (block - WINDOW) + j).wait_send()
+            row_copy(4 * block + j).start()
 
     def send_and_add(group):
         send_on(2 * group + WINDOW)
         send_on(2 * group + WINDOW + 1)
-        add(group)
+        add(group - 1)
 
     paired = (patches // 4 - WINDOW) // 2
-    each(0, paired, send_and_add)
-    each(paired, last, add)
+    pick(WINDOW)
+    for j in range(4):
+        if j:
+            row_copy(j).wait_send()
+        row_copy(4 * WINDOW + j).start()
+    send_on(WINDOW + 1)
+    each(1, paired, send_and_add)
+    each(paired - 1, last, add)
     for t in range(channels // tile):
         settle(t, total[tile * t : tile * (t + 1), :])
     each(8 * last, patches, lambda r: row_copy(r).wait_recv())
@@ -314,7 +321,7 @@
 
     def to_first(h):
         mine = bases.at[h, y, c, x, zl]
-        for o in (2, 1, 3, 0):
+        for o in (0, 2, 1, 3):
             for j in range(2):
                 if o + j:
                     to = {first[h]: ring(place[first[h]], o), "zl": 1 - zl if j else zl}

time: 125 us -> 126 us (level)
  no operation moved by 1% of the time
where the time goes in v12:
time: 126 us
  Pallas kernels  126 us (100%)
    pallas_call x1, Pallas kernels, cleaned(): pl.pallas_call(clean_kernel, out_shape=jax.ShapeDtypeStruct((pixels, chan...  123 us

profile of v12, /device:TPU:1, one launch (start us, length us, event | category | flops | bytes accessed | tf_op | source)
XLA Modules:
  0.0 125.5 jit_solution(5661387515122232101)
XLA Ops:
  0.0 123.1 %shard_map.55.from_ref = f32[512,1024]{1,0:T(8,128)} custom-call(s32[32,64]{1,0:T(8,128)} %bitcast.9, s32[1,64]{1,0:T(1,128)} %bitcast.11, f32[32,64]{1,0:T(8,128)} %bitcast.10, bf16[512,1024]{1,0:T(8,128)(2,1)} %sky_hbm.1, f32[12,1024]{1,0:T(8,128)} %bitcast.8), custom_call_target="tpu_custom_call" | custom-call | tf_op jit(solution)/shard_map/pallas_call | solution.py:401
  123.1 2.4 %shard_map.56 = f32[512,1024]{1,0:T(8,128)} custom-call(f32[512,1024]{1,0:T(8,128)} %shard_map.55.from_ref), custom_call_target="tpu_custom_call" | custom-call | tf_op jit(solution)/shard_map/pallas_call | solution.py:453

commit v13 on v12

--- a/solution.py
+++ b/solution.py
@@ -12,7 +12,7 @@
 MESH = pl.DeviceIdType.MESH
 MIB = 1 << 20
 VMEM_MIB = 56
-WINDOW = 4
+WINDOW = 6
 
 
 def two_pieces(value):

time: 126 us -> 126 us (level)
  no operation moved by 1% of the time
where the time goes in v13:
time: 126 us
  Pallas kernels  125 us (99%)
    pallas_call x1, Pallas kernels, cleaned(): pl.pallas_call(clean_kernel, out_shape=jax.ShapeDtypeStruct((pixels, chan...  123 us

profile of v13, /device:TPU:1, one launch (start us, length us, event | category | flops | bytes accessed | tf_op | source)
XLA Modules:
  0.0 125.6 jit_solution(18383244839922235668)
XLA Ops:
  0.0 123.0 %shard_map.55.from_ref = f32[512,1024]{1,0:T(8,128)} custom-call(s32[32,64]{1,0:T(8,128)} %bitcast.9, s32[1,64]{1,0:T(1,128)} %bitcast.11, f32[32,64]{1,0:T(8,128)} %bitcast.10, bf16[512,1024]{1,0:T(8,128)(2,1)} %sky_hbm.1, f32[12,1024]{1,0:T(8,128)} %bitcast.8), custom_call_target="tpu_custom_call" | custom-call | tf_op jit(solution)/shard_map/pallas_call | solution.py:401
  123.0 2.4 %shard_map.56 = f32[512,1024]{1,0:T(8,128)} custom-call(f32[512,1024]{1,0:T(8,128)} %shard_map.55.from_ref), custom_call_target="tpu_custom_call" | custom-call | tf_op jit(solution)/shard_map/pallas_call | solution.py:453

commit v14 on v11

--- a/solution.py
+++ b/solution.py
@@ -314,7 +314,7 @@
 
     def to_first(h):
         mine = bases.at[h, y, c, x, zl]
-        for o in (2, 1, 3, 0):
+        for o in (0, 2, 1, 3):
             for j in range(2):
                 if o + j:
                     to = {first[h]: ring(place[first[h]], o), "zl": 1 - zl if j else zl}
@@ -432,11 +432,13 @@
     parts = [pl.ds(count * i, count) for i in range(chunks)]
     loads = [pltpu.make_async_copy(from_ref.at[p], held.at[p], in_sem.at[i]) for i, p in enumerate(parts)]
     stores = [pltpu.make_async_copy(held.at[p], to_ref.at[p], out_sem.at[i]) for i, p in enumerate(parts)]
-    for load in loads:
+    for load in loads[:2]:
         load.start()
-    for load, store in zip(loads, stores):
-        load.wait()
-        store.start()
+    for i in range(chunks):
+        loads[i].wait()
+        stores[i].start()
+        if i + 2 < chunks:
+            loads[i + 2].start()
     for store in stores:
         store.wait()
 

time: 125 us -> 129 us (1.032)
  Pallas kernels: 125 us -> 128 us
    pallas_call x1, Pallas kernels: 2.39 us -> 5.28 us  [copied(): pl.pallas_call(copy_kernel, out_shape=jax.ShapeDtypeStruct(array.shape, a...]
where the time goes in v14:
time: 129 us; the launch traced here: 128 us
  Pallas kernels  128 us (99%)
    pallas_call x1, Pallas kernels, cleaned(): pl.pallas_call(clean_kernel, out_shape=jax.ShapeDtypeStruct((pixels, chan...  123 us
    pallas_call x1, Pallas kernels, copied(): pl.pallas_call(copy_kernel, out_shape=jax.ShapeDtypeStruct(array.shape, a...  5.28 us

profile of v14, /device:TPU:1, one launch (start us, length us, event | category | flops | bytes accessed | tf_op | source)
XLA Modules:
  0.0 128.4 jit_solution(7734762677035373978)
XLA Ops:
  0.0 123.1 %shard_map.55.from_ref = f32[512,1024]{1,0:T(8,128)} custom-call(s32[32,64]{1,0:T(8,128)} %bitcast.9, s32[1,64]{1,0:T(1,128)} %bitcast.11, f32[32,64]{1,0:T(8,128)} %bitcast.10, bf16[512,1024]{1,0:T(8,128)(2,1)} %sky_hbm.1, f32[12,1024]{1,0:T(8,128)} %bitcast.8), custom_call_target="tpu_custom_call" | custom-call | tf_op jit(solution)/shard_map/pallas_call | solution.py:394
  123.1 5.3 %shard_map.56 = f32[512,1024]{1,0:T(8,128)} custom-call(f32[512,1024]{1,0:T(8,128)} %shard_map.55.from_ref), custom_call_target="tpu_custom_call" | custom-call | tf_op jit(solution)/shard_map/pallas_call | solution.py:448
